TPU v7x, 128 devices: a whole 4x4x4 slice. The times are simulated.
128 devices in a mesh: azim: 16 (over x_hi, z, core), axial: 8 (over y, x_lo).
Axes of the slice: x: 4 (x_hi: 2, x_lo: 2; x = x_hi * 2 + x_lo), y: 4, z: 4, core: 2. Of those that a mesh axis runs over, the one named last changes fastest.
Arguments:
- flow_state: float32 [11, 4, 4, 4, 16, 64, 128], P(None, None, None, None, 'azim', 'axial'), may hold values from -6 to 6
- velocity: float32 [3, 4, 4, 4, 16, 64, 128], P(None, None, None, None, 'azim', 'axial'), may hold values from -3 to 3
- inlet_state: float32 [11, 4, 4, 16, 128], P(None, None, None, 'azim'), may hold values from -6 to 6
- radial_inflow: float32 [2, 11, 4, 4, 16, 64], P(None, None, None, None, 'azim', 'axial'), may hold values from -6 to 6
- face_tags: int32 [2, 16, 64], P(None, 'azim', 'axial'), may hold values from 0 to 2
- decay_rates: float32 [11], replicated, may hold values from 0.3 to 8
Outputs:
- next_state: float32 [11, 4, 4, 4, 16, 64, 128], P(None, None, None, None, 'azim', 'axial')
All inputs are finite; a program needn't handle non-finite values.
Results may differ from a plain program's by a relative error of at most 0.0001.
Values sent between devices are 32-bit elements; how exact they have to be, the bound alone decides.
No kernel may reach another device: no remote copies, remote signals or barrier semaphores. Data moves between devices by JAX's collectives and lax.ppermute only.
A program may use at most 128 MiB of HBM per device.

v0:
```python
import jax
import jax.numpy as jnp
import numpy as np
from jax import lax
from jax.experimental import pallas as pl
from jax.experimental.pallas import tpu as pltpu
from jax.sharding import PartitionSpec as P

time_step = 0.025
metric_scales = (2.0, 1.6, 2.4)
root5 = float(np.sqrt(5.0))
speed_scales = tuple(0.25 * c * time_step for c in metric_scales)
vmem = pl.BlockSpec(memory_space=pltpu.VMEM)
smem = pl.BlockSpec(memory_space=pltpu.SMEM)
anywhere = pl.BlockSpec(memory_space=pl.ANY)
vmem_limit = 40 * 1024 * 1024
tile = (8, 128)


def params():
    return pltpu.CompilerParams(vmem_limit_bytes=vmem_limit)


def arr(*shape):
    return jax.ShapeDtypeStruct(shape, jnp.float32)


def volume(g0, g1, g2, g3):
    e0, o0, e1, o1 = g0 + g3, g0 - g3, g1 + g2, g1 - g2
    h1 = root5 * o1
    s03 = o0 - 5.0 * h1
    d03 = e0 + 5.0 * e1
    s12 = o0 + h1
    d12 = root5 * (e0 - e1)
    return s03 - d03, s12 + d12, s12 - d12, s03 + d03


def face_planes():
    odd = lax.rem(lax.axis_index("azim"), 2)
    return 3 * odd, 3 - 3 * odd


def extract_kernel(u, vel, cross, chip, sems):
    plane_x, plane_c = face_planes()
    fields = u.shape[0]
    copies = []
    for dst, plane in ((cross, plane_x), (chip, plane_c)):
        copies.append((u.at[:, plane], dst.at[pl.ds(0, fields)]))
        copies.append((vel.at[0, plane], dst.at[fields]))
    copies = [pltpu.make_async_copy(s, d, sems.at[i]) for i, (s, d) in enumerate(copies)]
    for c in copies:
        c.start()
    for c in copies:
        c.wait()


def extract(u, vel):
    fields = u.shape[0]
    return pl.pallas_call(
        extract_kernel,
        out_shape=[arr(fields + 1, 16, 8, 128)] * 2,
        in_specs=[anywhere] * 2,
        out_specs=[anywhere] * 2,
        scratch_shapes=[pltpu.SemaphoreType.DMA((4,))],
        compiler_params=params(),
    )(u, vel)


def speeds_and_coefs(vel, tags, va, cax, crad, ghost_l, ghost_r):
    fields = ghost_l.shape[0] - 1
    lane = lax.broadcasted_iota(jnp.int32, tile, 1)
    sub = lax.broadcasted_iota(jnp.int32, tile, 0)
    position = lax.axis_index("axial")
    first = jnp.logical_and(sub == 0, position == 0)
    last = jnp.logical_and(sub == 7, position == lax.axis_size("axial") - 1)
    tag = tags[...]
    inner, outer = lane == 0, lane == 127

    def plane(a, carry):
        for d in range(3):
            for k in range(16):
                va[d, a, k] = vel[d, a, k] * speed_scales[d]
        for r in range(4):
            a0, a3 = va[1, a, r], va[1, a, 12 + r]
            row_l = ghost_l[fields, pl.ds(a * 4 + r, 1), :] * speed_scales[1]
            row_r = ghost_r[fields, pl.ds(a * 4 + r, 1), :] * speed_scales[1]
            below = jnp.where(sub == 0, row_l, pltpu.roll(a3, 1, 0))
            below = jnp.where(first, a0, below)
            above = jnp.where(sub == 7, row_r, pltpu.roll(a0, 7, 0))
            m_low = jnp.maximum(jnp.abs(a0), jnp.abs(below))
            m_up = jnp.maximum(jnp.abs(a3), jnp.abs(above))
            cax[a, r, 0] = -12.0 * m_low
            cax[a, r, 1] = 12.0 * (m_low + below)
            cax[a, r, 2] = jnp.where(last, -12.0 * a3, -12.0 * m_up)
            cax[a, r, 3] = jnp.where(last, 0.0, 12.0 * (m_up - above))
        for x in range(4):
            a0, a3 = va[2, a, 4 * x], va[2, a, 4 * x + 3]
            below = jnp.where(inner, a0, pltpu.roll(a3, 1, 1))
            above = jnp.where(outer, a3, pltpu.roll(a0, 127, 1))
            m_low = jnp.maximum(jnp.abs(a0), jnp.abs(below))
            m_up = jnp.maximum(jnp.abs(a3), jnp.abs(above))
            own_low, out_low = -12.0 * m_low, 12.0 * (m_low + below)
            own_up, out_up = -12.0 * m_up, 12.0 * (m_up - above)
            own_low = jnp.where(inner & (tag == 0), -12.0 * a0, own_low)
            own_low = jnp.where(inner & (tag == 2), 12.0 * a0, own_low)
            own_up = jnp.where(outer & (tag == 0), 12.0 * a3, own_up)
            own_up = jnp.where(outer & (tag == 2), -12.0 * a3, own_up)
            closed = (inner | outer) & (tag != 1)
            crad[a, x, 0] = own_low
            crad[a, x, 1] = jnp.where(inner & closed, 0.0, out_low)
            crad[a, x, 2] = own_up
            crad[a, x, 3] = jnp.where(outer & closed, 0.0, out_up)
        return carry

    lax.fori_loop(0, 4, plane, 0)


def plane_terms(f, a, keep, src, va, cax, crad, edge, ghost_l, ghost_r, edge_f):
    lane = lax.broadcasted_iota(jnp.int32, tile, 1)
    sub = lax.broadcasted_iota(jnp.int32, tile, 0)
    u = [src[f, a, k] for k in range(16)]
    acc = [keep * v for v in u]
    for r in range(4):
        line = [u[4 * x + r] for x in range(4)]
        out = volume(*[va[1, a, 4 * x + r] * line[x] for x in range(4)])
        below = jnp.where(
            sub == 0, ghost_l[edge_f, pl.ds(a * 4 + r, 1), :], pltpu.roll(line[3], 1, 0)
        )
        above = jnp.where(
            sub == 7, ghost_r[edge_f, pl.ds(a * 4 + r, 1), :], pltpu.roll(line[0], 7, 0)
        )
        acc[r] += out[0] + (cax[a, r, 0] * line[0] + cax[a, r, 1] * below)
        acc[4 + r] += out[1]
        acc[8 + r] += out[2]
        acc[12 + r] += out[3] + (cax[a, r, 2] * line[3] + cax[a, r, 3] * above)
    for x in range(4):
        line = [u[4 * x + r] for r in range(4)]
        out = volume(*[va[2, a, 4 * x + r] * line[r] for r in range(4)])
        imposed = edge[edge_f, a * 4 + x]
        below = jnp.where(lane == 0, imposed, pltpu.roll(line[3], 1, 1))
        above = jnp.where(lane == 127, imposed, pltpu.roll(line[0], 127, 1))
        acc[4 * x] += out[0] + (crad[a, x, 0] * line[0] + crad[a, x, 1] * below)
        acc[4 * x + 1] += out[1]
        acc[4 * x + 2] += out[2]
        acc[4 * x + 3] += out[3] + (crad[a, x, 2] * line[3] + crad[a, x, 3] * above)
    return u, acc


def pack_ghosts(inlet, recv_a, recv_b, ghost_l, ghost_r):
    position = lax.axis_index("axial")
    odd = lax.rem(position, 2) == 1
    rows = recv_a.shape[0]
    fields = inlet.shape[0]
    a, b = recv_a[...], recv_b[...]
    lower = jnp.where(odd, a, b)
    ghost_r[pl.ds(0, rows)] = jnp.where(odd, b, a)
    ghost_l[pl.ds(0, fields)] = jnp.where(position == 0, inlet[...], lower[:fields])
    if rows > fields:
        ghost_l[fields] = lower[fields]


def first_kernel(
    decay, tags, edge, inlet, recv_a, recv_b, u, vel, acc, va, cax, crad, ghost_l, ghost_r
):
    fields = u.shape[0]
    pack_ghosts(inlet, recv_a, recv_b, ghost_l, ghost_r)
    speeds_and_coefs(vel, tags, va, cax, crad, ghost_l, ghost_r)

    def field(f, carry):
        keep = 1.0 - time_step * decay[f]

        def plane(a, carry):
            _, out = plane_terms(f, a, keep, u, va, cax, crad, edge, ghost_l, ghost_r, f)
            for k in range(16):
                acc[f, a, k] = out[k]
            return carry

        lax.fori_loop(0, 4, plane, 0)

        def lines(q, carry):
            for r in range(4):
                k = q * 4 + r
                out = volume(*[va[0, a, k] * u[f, a, k] for a in range(4)])
                for a in range(4):
                    acc[f, a, k] += out[a]
            return carry

        lax.fori_loop(0, 4, lines, 0)
        return carry

    lax.fori_loop(0, fields, field, 0)


def first_section(decay, tags, edge, inlet, recv_a, recv_b, u, vel):
    fields = u.shape[0]
    return pl.pallas_call(
        first_kernel,
        out_shape=[
            arr(fields, 4, 16, 8, 128),
            arr(3, 4, 16, 8, 128),
            arr(4, 4, 4, 8, 128),
            arr(4, 4, 4, 8, 128),
        ],
        in_specs=[smem] + [vmem] * 7,
        out_specs=[vmem] * 4,
        scratch_shapes=[pltpu.VMEM((fields + 1, 16, 128), jnp.float32)] * 2,
        compiler_params=params(),
    )(decay, tags, edge, inlet, recv_a, recv_b, u, vel)


def close_kernel(recv_x, recv_c, u, va, acc, s1, send_x, send_c, send_a, send_b, caz):
    fields = u.shape[0]
    planes = face_planes()
    for side, (recv, send) in enumerate(((recv_x, send_x), (recv_c, send_c))):
        plane = planes[side]
        sign = jnp.where(plane == 0, 1.0, -1.0)
        for k in range(16):
            own, other = va[0, plane, k], recv[fields, k] * speed_scales[0]
            m = jnp.maximum(jnp.abs(own), jnp.abs(other))
            caz[plane, k] = -12.0 * m
            caz[plane + 1 - lax.div(plane, 3) * 2, k] = 12.0 * (m + sign * other)

    position = lax.axis_index("axial")
    odd = lax.rem(position, 2) == 1

    def field(f, carry):
        for side, (recv, send) in enumerate(((recv_x, send_x), (recv_c, send_c))):
            plane = planes[side]
            beside = plane + 1 - lax.div(plane, 3) * 2
            for k in range(16):
                value = acc[f, plane, k] + (
                    caz[plane, k] * u[f, plane, k] + caz[beside, k] * recv[f, k]
                )
                s1[f, plane, k] = value
                send[f, k] = value
        for a in (1, 2):
            for k in range(16):
                s1[f, a, k] = acc[f, a, k]
        for a in range(4):
            for r in range(4):
                low = s1[f, a, r, pl.ds(0, 1), :]
                high = s1[f, a, 12 + r, pl.ds(7, 1), :]
                send_a[f, pl.ds(a * 4 + r, 1), :] = jnp.where(odd, low, high)
                send_b[f, pl.ds(a * 4 + r, 1), :] = jnp.where(odd, high, low)
        return carry

    lax.fori_loop(0, fields, field, 0)


def close_first(recv_x, recv_c, u, va, acc):
    fields = u.shape[0]
    return pl.pallas_call(
        close_kernel,
        out_shape=[
            arr(fields, 4, 16, 8, 128),
            arr(fields, 16, 8, 128),
            arr(fields, 16, 8, 128),
            arr(fields, 16, 128),
            arr(fields, 16, 128),
            arr(4, 16, 8, 128),
        ],
        in_specs=[vmem] * 5,
        out_specs=[vmem] * 6,
        compiler_params=params(),
    )(recv_x, recv_c, u, va, acc)


def second_kernel(
    decay, edge, inlet, recv_a, recv_b, u, s1, va, cax, crad, caz, part, ghost_l, ghost_r
):
    fields = u.shape[0]
    pack_ghosts(inlet, recv_a, recv_b, ghost_l, ghost_r)

    def field(f, carry):
        keep = 1.0 - time_step * decay[f]

        def plane(a, carry):
            _, out = plane_terms(f, a, keep, s1, va, cax, crad, edge, ghost_l, ghost_r, f)
            for k in range(16):
                part[f, a, k] = 0.5 * (u[f, a, k] + out[k])
            return carry

        lax.fori_loop(0, 4, plane, 0)

        def lines(q, carry):
            for r in range(4):
                k = q * 4 + r
                line = [s1[f, a, k] for a in range(4)]
                out = list(volume(*[va[0, a, k] * line[a] for a in range(4)]))
                out[0] += caz[0, k] * line[0]
                out[3] += caz[3, k] * line[3]
                for a in range(4):
                    part[f, a, k] += 0.5 * out[a]
            return carry

        lax.fori_loop(0, 4, lines, 0)
        return carry

    lax.fori_loop(0, fields, field, 0)


def second_section(decay, edge, inlet, recv_a, recv_b, u, s1, va, cax, crad, caz):
    fields = u.shape[0]
    return pl.pallas_call(
        second_kernel,
        out_shape=arr(fields, 4, 16, 8, 128),
        in_specs=[smem] + [vmem] * 10,
        out_specs=vmem,
        scratch_shapes=[pltpu.VMEM((fields, 16, 128), jnp.float32)] * 2,
        compiler_params=params(),
    )(decay, edge, inlet, recv_a, recv_b, u, s1, va, cax, crad, caz)


def finish_kernel(recv_x, recv_c, caz, part, out):
    fields = part.shape[0]
    planes = face_planes()

    def field(f, carry):
        for side, recv in enumerate((recv_x, recv_c)):
            plane = planes[side]
            beside = plane + 1 - lax.div(plane, 3) * 2
            for k in range(16):
                out[f, plane, k] = part[f, plane, k] + 0.5 * (caz[beside, k] * recv[f, k])
        for a in (1, 2):
            for k in range(16):
                out[f, a, k] = part[f, a, k]
        return carry

    lax.fori_loop(0, fields, field, 0)


def finish(recv_x, recv_c, caz, part):
    return pl.pallas_call(
        finish_kernel,
        out_shape=arr(*part.shape),
        in_specs=[vmem] * 4,
        out_specs=vmem,
        compiler_params=params(),
    )(recv_x, recv_c, caz, part)


def swap(array, axis, odd_up):
    count = lax.axis_size(axis)
    if odd_up:
        route = [(i, (i + 1) % count if i % 2 else (i - 1) % count) for i in range(count)]
    else:
        route = [(i, i ^ 1) for i in range(count)]
    return lax.ppermute(array, axis, route)


def per_device(flow_state, velocity, inlet_state, radial_inflow, face_tags, decay_rates):
    fields = flow_state.shape[0]
    u = flow_state.reshape((fields, 4, 16) + tile)
    vel = velocity.reshape((3, 4, 16) + tile)
    inlet = inlet_state.reshape(fields, 16, 128)
    lane = lax.broadcasted_iota(jnp.int32, tile, 1)
    tags = jnp.where(lane == 0, face_tags[0].reshape(8, 1), face_tags[1].reshape(8, 1))
    edges = radial_inflow.reshape(2, fields, 16, 8, 1)
    edge = jnp.where(lane == 0, edges[0], edges[1])

    send_x, send_c = extract(u, vel)
    odd = lax.rem(lax.axis_index("axial"), 2) == 1
    stack = jnp.concatenate(
        [flow_state[:, :, :, :, 0], velocity[1:2, :, :, :, 0]], 0
    )
    low = stack[:, :, 0, :, 0, :].reshape(fields + 1, 16, 128)
    high = stack[:, :, 3, :, 7, :].reshape(fields + 1, 16, 128)
    send_a = jnp.where(odd, low, high)
    send_b = jnp.where(odd, high, low)

    recv_x = swap(send_x, "azim", True)
    recv_c = swap(send_c, "azim", False)
    recv_a = swap(send_a, "axial", False)
    recv_b = swap(send_b, "axial", True)

    acc, va, cax, crad = first_section(
        decay_rates, tags, edge, inlet, recv_a, recv_b, u, vel
    )
    s1, send_x, send_c, send_a, send_b, caz = close_first(recv_x, recv_c, u, va, acc)

    recv_x = swap(send_x, "azim", True)
    recv_c = swap(send_c, "azim", False)
    recv_a = swap(send_a, "axial", False)
    recv_b = swap(send_b, "axial", True)

    part = second_section(
        decay_rates, edge, inlet, recv_a, recv_b, u, s1, va, cax, crad, caz
    )
    out = finish(recv_x, recv_c, caz, part)
    return out.reshape(flow_state.shape)


def solution(mesh):
    in_specs = (
        P(None, None, None, None, "azim", "axial", None),
        P(None, None, None, None, "azim", "axial", None),
        P(None, None, None, "azim", None),
        P(None, None, None, None, "azim", "axial"),
        P(None, "azim", "axial"),
        P(),
    )
    out_specs = P(None, None, None, None, "azim", "axial", None)
    return jax.shard_map(
        per_device, mesh=mesh, in_specs=in_specs, out_specs=out_specs, check_vma=False
    )
```

profile of v0, /device:TPU:0, one launch (start us, length us, event | category | flops | bytes accessed | tf_op | source)
XLA Modules:
  0.0 53.1 jit_solution(5723131435776753967)
XLA Ops:
  0.0 0.0 copy-start
  0.0 0.0 copy-start.1
  0.0 1.1 %slice_bitcast_fusion = f32[1,4,4,4,8,128]{5,4,3,2,1,0:T(8,128)S(1)} fusion(f32[3,4,4,4,1,8,128]{6,5,4,3,2,1,0:T(8,128)} %param.7), kind=kLoop, calls=%fused_computation.1 | loop fusion | bytes 524288 | tf_op jit(solution)/shard_map/squeeze | solution.py:364
  1.1 0.0 copy-start.5
  1.1 1.6 %broadcast_select_fusion.1 = (f32[12,4,1,4,1,128]{5,4,3,2,1,0:T(1,128)S(1)}, f32[12,4,1,4,1,128]{5,4,3,2,1,0:T(1,128)S(1)}, f32[12,4,1,4,1,128]{5,4,3,2,1,0:T(1,128)S(1)}) fusion(pred[]{:T(512)S(6)} %eq.11, f32[1,4,4,4,8,128]{5,4,3,2,1,0:T(8,128)S(1)} %slice_bitcast_fusion, f32[11,4,4,4,8,128]{5,4,3,2,1,0:T(8,128)} %bitcast.17), kind=kLoop, calls=%fused_computation.2 | loop fusion | flops 73728 | bytes 3440641 | tf_op jit(solution)/shard_map/jit(_where)/select_n | solution.py:369
  2.7 0.0 copy-start.6
  2.8 0.0 copy-start.3
  2.8 0.0 copy-start.4
  2.8 0.7 %broadcast_select_fusion.2 = f32[12,4,1,4,1,128]{5,4,3,2,1,0:T(1,128)} fusion(f32[12,4,1,4,1,128]{5,4,3,2,1,0:T(1,128)S(1)} %get-tuple-element.31, f32[12,4,1,4,1,128]{5,4,3,2,1,0:T(1,128)S(1)} %get-tuple-element.30, pred[]{:T(512)S(6)} %eq.11), kind=kLoop, calls=%fused_computation.3 | loop fusion | flops 24576 | bytes 294913 | tf_op jit(solution)/shard_map/jit(_where)/select_n | solution.py:368
  3.5 1.6 %collective-permute-start.2 = (f32[12,16,128]{2,1,0:T(8,128)}, f32[12,16,128]{2,1,0:T(8,128)S(1)}, u32[]{:S(2)}, u32[]{:S(2)}) collective-permute-start(f32[12,16,128]{2,1,0:T(8,128)} %bitcast.9), channel_id=1, source_target_pairs={{0,1},{1,0},{2,3},{3,2},{4,5},{5,4},{6,7},{7,6},{8,9},{9,8},{10,11... | collective-permute-start | bytes 294920 | tf_op jit(solution)/shard_map/ppermute | solution.py:348
  5.1 3.0 %collective-permute-start.3 = (f32[12,16,128]{2,1,0:T(8,128)S(1)}, f32[12,16,128]{2,1,0:T(8,128)S(1)}, u32[]{:S(2)}, u32[]{:S(2)}) collective-permute-start(f32[12,16,128]{2,1,0:T(8,128)S(1)} %bitcast.28), channel_id=1, source_target_pairs={{0,7},{1,2},{2,1},{3,4},{4,3},{5,6},{6,5},{7,0},{8,15},{9,10},{10,... | collective-permute-start | bytes 294920 | tf_op jit(solution)/shard_map/ppermute | solution.py:348
  8.1 0.0 copy-done
  8.1 0.0 copy-done.1
  8.1 1.2 %shard_map.64 = (f32[12,16,8,128]{3,2,1,0:T(8,128)}, f32[12,16,8,128]{3,2,1,0:T(8,128)}) custom-call(f32[11,4,16,8,128]{4,3,2,1,0:T(8,128)S(1)} %bitcast.18, f32[3,4,16,8,128]{4,3,2,1,0:T(8,128)S(1)} %bitcast.22), custom_call_target="tpu_custom_call" | custom-call | tf_op jit(solution)/shard_map/pallas_call | solution.py:59
  9.3 5.5 %collective-permute-start = (f32[12,16,8,128]{3,2,1,0:T(8,128)}, f32[12,16,8,128]{3,2,1,0:T(8,128)}, u32[]{:S(2)}, u32[]{:S(2)}) collective-permute-start(f32[12,16,8,128]{3,2,1,0:T(8,128)} %get-tuple-element.17), channel_id=1, source_target_pairs={{0,120},{8,16},{16,8},{24,32},{32,24},{40,48},{48,40},{56,64},{64,... | collective-permute-start | bytes 2359304 | tf_op jit(solution)/shard_map/ppermute | solution.py:348
  14.7 0.0 collective-permute-start.1
  14.7 0.0 copy-done.5
  14.7 0.2 copy.8
  14.9 0.2 copy.7
  15.1 0.0 copy-done.6
  15.1 0.4 broadcast_select_fusion.edge
  15.6 0.1 broadcast_select_fusion.3.tags
  15.6 0.0 collective-permute-done.2.recv_a
  15.6 0.0 collective-permute-done.3.recv_b
  15.6 0.0 copy-done.3
  15.7 0.0 copy-done.4
  15.7 0.0 copy-start.2
  15.7 1.1 %copy-done.2 = f32[3,4,4,4,1,8,128]{6,5,4,3,2,1,0:T(8,128)S(1)} copy-done((f32[3,4,4,4,1,8,128]{6,5,4,3,2,1,0:T(8,128)S(1)}, f32[3,4,4,4,1,8,128]{6,5,4,3,2,1,0:T(8,128)}, u32[]{:S(2)}) %copy-start.2) | copy-done | bytes 786456
  16.8 5.5 %shard_map.65 = (f32[11,4,16,8,128]{4,3,2,1,0:T(8,128)S(1)}, f32[3,4,16,8,128]{4,3,2,1,0:T(8,128)S(1)}, f32[4,4,4,8,128]{4,3,2,1,0:T(8,128)S(1)}, f32[4,4,4,8,128]{4,3,2,1,0:T(8,128)S(1)}) custom-call(f32[11]{0:T(128)S(1)} %copy-done.4, s32[8,128]{1,0:T(8,128)S(1)} %broadcast_select_fusion.3.tags, f32[11,16,8,128]{3,2,1,0:T(8,128)S(1)} %broadcast_select_fusion.edge, ...), custom_call_target="tpu_custom_call" | custom-call | tf_op jit(solution)/shard_map/pallas_call | solution.py:196
  22.3 3.4 %collective-permute-done.recv_x = f32[12,16,8,128]{3,2,1,0:T(8,128)} collective-permute-done((f32[12,16,8,128]{3,2,1,0:T(8,128)}, f32[12,16,8,128]{3,2,1,0:T(8,128)}, u32[]{:S(2)}, u32[]{:S(2)}) %collective-permute-start) | collective-permute-done | bytes 786464 | tf_op jit(solution)/shard_map/ppermute | solution.py:348
  25.7 0.0 collective-permute-done.1.recv_c
  25.7 2.0 %shard_map.66 = (f32[11,4,16,8,128]{4,3,2,1,0:T(8,128)S(1)}, f32[11,16,8,128]{3,2,1,0:T(8,128)S(1)}, f32[11,16,8,128]{3,2,1,0:T(8,128)S(1)}, f32[11,16,128]{2,1,...) custom-call(f32[12,16,8,128]{3,2,1,0:T(8,128)} %collective-permute-done.recv_x, ...), custom_call_target="tpu_custom_call" | custom-call | tf_op jit(solution)/shard_map/pallas_call | solution.py:252
  27.8 4.5 %collective-permute-start.4 = (f32[11,16,8,128]{3,2,1,0:T(8,128)S(1)}, f32[11,16,8,128]{3,2,1,0:T(8,128)S(1)}, u32[]{:S(2)}, u32[]{:S(2)}) collective-permute-start(f32[11,16,8,128]{3,2,1,0:T(8,128)S(1)} %get-tuple-element.21), channel_id=1, source_target_pairs={{0,120},{8,16},{16,8},{24,32},{32,24},{40,48},{48,40},{56,64},{64,... | collective-permute-start | bytes 2162696 | tf_op jit(solution)/shard_map/ppermute | solution.py:348
  32.2 0.0 collective-permute-start.5
  32.2 0.0 collective-permute-start.6
  32.2 2.2 %collective-permute-start.7 = (f32[11,16,128]{2,1,0:T(8,128)S(1)}, f32[11,16,128]{2,1,0:T(8,128)S(1)}, u32[]{:S(2)}, u32[]{:S(2)}) collective-permute-start(f32[11,16,128]{2,1,0:T(8,128)S(1)} %get-tuple-element.25), channel_id=1, source_target_pairs={{0,7},{1,2},{2,1},{3,4},{4,3},{5,6},{6,5},{7,0},{8,15},{9,10},{10,... | collective-permute-start | bytes 270344 | tf_op jit(solution)/shard_map/ppermute | solution.py:348
  34.4 9.3 %collective-permute-done.6.recv_a = f32[11,16,128]{2,1,0:T(8,128)S(1)} collective-permute-done((f32[11,16,128]{2,1,0:T(8,128)S(1)}, f32[11,16,128]{2,1,0:T(8,128)S(1)}, u32[]{:S(2)}, u32[]{:S(2)}) %collective-permute-start.6) | collective-permute-done | bytes 90144 | tf_op jit(solution)/shard_map/ppermute | solution.py:348
  43.7 1.8 %collective-permute-done.7.recv_b = f32[11,16,128]{2,1,0:T(8,128)S(1)} collective-permute-done((f32[11,16,128]{2,1,0:T(8,128)S(1)}, f32[11,16,128]{2,1,0:T(8,128)S(1)}, u32[]{:S(2)}, u32[]{:S(2)}) %collective-permute-start.7) | collective-permute-done | bytes 90144 | tf_op jit(solution)/shard_map/ppermute | solution.py:348
  45.6 5.4 %shard_map.67.part = f32[11,4,16,8,128]{4,3,2,1,0:T(8,128)S(1)} custom-call(f32[11]{0:T(128)S(1)} %copy-done.4, f32[11,16,8,128]{3,2,1,0:T(8,128)S(1)} %broadcast_select_fusion.edge, f32[11,16,128]{2,1,0:T(8,128)S(1)} %bitcast.25, f32[11,16,128]{2,1,0:T(8,128)S(1)} %collective-permute-done.6.recv_a, f32[11,16,128]{2,1,0:T(8,128)S(1)} %collective-permute-done.7.recv_b, ...), custom_call_target="tpu_custom_call" | custom-call | tf_op jit(solution)/shard_map/pallas_call | solution.py:304
  51.0 0.0 collective-permute-done.4.recv_x
  51.0 0.0 collective-permute-done.5.recv_c
  51.1 2.0 %shard_map.68 = f32[11,4,16,8,128]{4,3,2,1,0:T(8,128)} custom-call(f32[11,16,8,128]{3,2,1,0:T(8,128)S(1)} %collective-permute-done.4.recv_x, f32[11,16,8,128]{3,2,1,0:T(8,128)S(1)} %collective-permute-done.5.recv_c, f32[4,16,8,128]{3,2,1,0:T(8,128)S(1)} %get-tuple-element.23.caz, f32[11,4,16,8,128]{4,3,2,1,0:T(8,128)S(1)} %shard_map.67.part), custom_call_target="tpu_custom_call" | custom-call | tf_op jit(solution)/shard_map/pallas_call | solution.py:333
  (3 shorter events, 0.0 us)
Async XLA Ops:
  0.0 8.1 %copy-start = (f32[11,4,4,4,1,8,128]{6,5,4,3,2,1,0:T(8,128)S(1)}, f32[11,4,4,4,1,8,128]{6,5,4,3,2,1,0:T(8,128)}, u32[]{:S(2)}) copy-start(f32[11,4,4,4,1,8,128]{6,5,4,3,2,1,0:T(8,128)} %param.6) | copy-start | bytes 8650756
  0.0 8.1 %copy-start.1 = (f32[3,4,4,4,1,8,128]{6,5,4,3,2,1,0:T(8,128)S(1)}, f32[3,4,4,4,1,8,128]{6,5,4,3,2,1,0:T(8,128)}, u32[]{:S(2)}) copy-start(f32[3,4,4,4,1,8,128]{6,5,4,3,2,1,0:T(8,128)} %param.7) | copy-start | bytes 2359300
  1.1 13.6 %copy-start.5 = (f32[2,11,4,4,1,8]{1,5,4,3,2,0:T(8,128)S(1)}, f32[2,11,4,4,1,8]{1,5,4,3,2,0:T(8,128)}, u32[]{:S(2)}) copy-start(f32[2,11,4,4,1,8]{1,5,4,3,2,0:T(8,128)} %param.9) | copy-start | bytes 33796
  2.7 12.4 %copy-start.6 = (s32[2,1,8]{2,1,0:T(1,128)S(1)}, s32[2,1,8]{2,1,0:T(1,128)}, u32[]{:S(2)}) copy-start(s32[2,1,8]{2,1,0:T(1,128)} %param.10) | copy-start | bytes 196
  2.8 12.9 %copy-start.3 = (f32[11,4,4,1,128]{4,3,2,1,0:T(1,128)S(1)}, f32[11,4,4,1,128]{4,3,2,1,0:T(1,128)}, u32[]{:S(2)}) copy-start(f32[11,4,4,1,128]{4,3,2,1,0:T(1,128)} %param.8) | copy-start | bytes 270340
  2.8 12.9 %copy-start.4 = (f32[11]{0:T(128)S(1)}, f32[11]{0:T(128)}, u32[]{:S(2)}) copy-start(f32[11]{0:T(128)} %decay.3) | copy-start | bytes 136
  3.5 12.1 %collective-permute-start.2 = (f32[12,16,128]{2,1,0:T(8,128)}, f32[12,16,128]{2,1,0:T(8,128)S(1)}, u32[]{:S(2)}, u32[]{:S(2)}) collective-permute-start(f32[12,16,128]{2,1,0:T(8,128)} %bitcast.9), channel_id=1, source_target_pairs={{0,1},{1,0},{2,3},{3,2},{4,5},{5,4},{6,7},{7,6},{8,9},{9,8},{10,11... | collective-permute-start | bytes 294920 | tf_op jit(solution)/shard_map/ppermute | solution.py:348
  5.1 10.6 %collective-permute-start.3 = (f32[12,16,128]{2,1,0:T(8,128)S(1)}, f32[12,16,128]{2,1,0:T(8,128)S(1)}, u32[]{:S(2)}, u32[]{:S(2)}) collective-permute-start(f32[12,16,128]{2,1,0:T(8,128)S(1)} %bitcast.28), channel_id=1, source_target_pairs={{0,7},{1,2},{2,1},{3,4},{4,3},{5,6},{6,5},{7,0},{8,15},{9,10},{10,... | collective-permute-start | bytes 294920 | tf_op jit(solution)/shard_map/ppermute | solution.py:348
  9.3 16.4 %collective-permute-start = (f32[12,16,8,128]{3,2,1,0:T(8,128)}, f32[12,16,8,128]{3,2,1,0:T(8,128)}, u32[]{:S(2)}, u32[]{:S(2)}) collective-permute-start(f32[12,16,8,128]{3,2,1,0:T(8,128)} %get-tuple-element.17), channel_id=1, source_target_pairs={{0,120},{8,16},{16,8},{24,32},{32,24},{40,48},{48,40},{56,64},{64,... | collective-permute-start | bytes 2359304 | tf_op jit(solution)/shard_map/ppermute | solution.py:348
  14.7 11.0 %collective-permute-start.1 = (f32[12,16,8,128]{3,2,1,0:T(8,128)}, f32[12,16,8,128]{3,2,1,0:T(8,128)}, u32[]{:S(2)}, u32[]{:S(2)}) collective-permute-start(f32[12,16,8,128]{3,2,1,0:T(8,128)} %get-tuple-element.18), channel_id=1, source_target_pairs={{0,8},{8,0},{16,24},{24,16},{32,40},{40,32},{48,56},{56,48},{64,72... | collective-permute-start | bytes 2359304 | tf_op jit(solution)/shard_map/ppermute | solution.py:348
  15.7 1.1 %copy-start.2 = (f32[3,4,4,4,1,8,128]{6,5,4,3,2,1,0:T(8,128)S(1)}, f32[3,4,4,4,1,8,128]{6,5,4,3,2,1,0:T(8,128)}, u32[]{:S(2)}) copy-start(f32[3,4,4,4,1,8,128]{6,5,4,3,2,1,0:T(8,128)} %param.7) | copy-start | bytes 2359300
  27.8 23.3 %collective-permute-start.4 = (f32[11,16,8,128]{3,2,1,0:T(8,128)S(1)}, f32[11,16,8,128]{3,2,1,0:T(8,128)S(1)}, u32[]{:S(2)}, u32[]{:S(2)}) collective-permute-start(f32[11,16,8,128]{3,2,1,0:T(8,128)S(1)} %get-tuple-element.21), channel_id=1, source_target_pairs={{0,120},{8,16},{16,8},{24,32},{32,24},{40,48},{48,40},{56,64},{64,... | collective-permute-start | bytes 2162696 | tf_op jit(solution)/shard_map/ppermute | solution.py:348
  32.2 18.8 %collective-permute-start.5 = (f32[11,16,8,128]{3,2,1,0:T(8,128)S(1)}, f32[11,16,8,128]{3,2,1,0:T(8,128)S(1)}, u32[]{:S(2)}, u32[]{:S(2)}) collective-permute-start(f32[11,16,8,128]{3,2,1,0:T(8,128)S(1)} %get-tuple-element.22), channel_id=1, source_target_pairs={{0,8},{8,0},{16,24},{24,16},{32,40},{40,32},{48,56},{56,48},{64,72... | collective-permute-start | bytes 2162696 | tf_op jit(solution)/shard_map/ppermute | solution.py:348
  32.2 11.5 %collective-permute-start.6 = (f32[11,16,128]{2,1,0:T(8,128)S(1)}, f32[11,16,128]{2,1,0:T(8,128)S(1)}, u32[]{:S(2)}, u32[]{:S(2)}) collective-permute-start(f32[11,16,128]{2,1,0:T(8,128)S(1)} %get-tuple-element.24), channel_id=1, source_target_pairs={{0,1},{1,0},{2,3},{3,2},{4,5},{5,4},{6,7},{7,6},{8,9},{9,8},{10,11... | collective-permute-start | bytes 270344 | tf_op jit(solution)/shard_map/ppermute | solution.py:348
  32.2 13.4 %collective-permute-start.7 = (f32[11,16,128]{2,1,0:T(8,128)S(1)}, f32[11,16,128]{2,1,0:T(8,128)S(1)}, u32[]{:S(2)}, u32[]{:S(2)}) collective-permute-start(f32[11,16,128]{2,1,0:T(8,128)S(1)} %get-tuple-element.25), channel_id=1, source_target_pairs={{0,7},{1,2},{2,1},{3,4},{4,3},{5,6},{6,5},{7,0},{8,15},{9,10},{10,... | collective-permute-start | bytes 270344 | tf_op jit(solution)/shard_map/ppermute | solution.py:348
where the time goes:
time: 53.2 us; the launch traced here: 53.1 us
  starting transfers between devices  16.7 us (31%)
  Pallas kernels  16.2 us (30%)
  waiting for transfers between devices  14.5 us (27%)
  other arithmetic  2.85 us (5%)
  local copies, waits for them, and re-layouts  2.64 us (5%)
    ppermute x8, starting transfers between devices, swap(): return lax.ppermute(array, axis, route)  16.7 us
    ppermute x8, waiting for transfers between devices, swap(): return lax.ppermute(array, axis, route)  14.5 us
    pallas_call x1, Pallas kernels, first_section(): pl.pallas_call(first_kernel, out_shape=[arr(fields, 4, 16, 8, 128), arr(3...  5.53 us
    pallas_call x1, Pallas kernels, second_section(): pl.pallas_call(second_kernel, out_shape=arr(fields, 4, 16, 8, 128), in_sp...  5.44 us
    pallas_call x1, Pallas kernels, close_first(): pl.pallas_call(close_kernel, out_shape=[arr(fields, 4, 16, 8, 128), arr(f...  2.05 us
    pallas_call x1, Pallas kernels, finish(): pl.pallas_call(finish_kernel, out_shape=arr(*part.shape), in_specs=[vmem]...  2.01 us
    select_n x1, other arithmetic, per_device(): send_b = jnp.where(odd, high, low)  1.6 us
    pallas_call x1, Pallas kernels, extract(): pl.pallas_call(extract_kernel, out_shape=[arr(fields + 1, 16, 8, 128)] *...  1.18 us
  transfers between devices with their start and end apart: 8, of which 3 were waited for; matrix products, arithmetic and copies ran while one was open for 2% of the time, Pallas kernels for 23%

commit v1 on v0

v1 whole, which is shorter than its diff:
```python
import jax
import jax.numpy as jnp
import numpy as np
from jax import lax
from jax.experimental import pallas as pl
from jax.experimental.pallas import tpu as pltpu
from jax.sharding import PartitionSpec as P

time_step = 0.025
metric_scales = (2.0, 1.6, 2.4)
root5 = float(np.sqrt(5.0))
speed_scales = tuple(0.25 * c * time_step for c in metric_scales)
vmem = pl.BlockSpec(memory_space=pltpu.VMEM)
smem = pl.BlockSpec(memory_space=pltpu.SMEM)
anywhere = pl.BlockSpec(memory_space=pl.ANY)
in_hbm = pl.BlockSpec(memory_space=pltpu.HBM)
vmem_limit = 40 * 1024 * 1024
tile = (8, 128)


def params(limit=vmem_limit):
    return pltpu.CompilerParams(vmem_limit_bytes=limit)


def arr(*shape):
    return jax.ShapeDtypeStruct(shape, jnp.float32)


def volume(g0, g1, g2, g3):
    e0, o0, e1, o1 = g0 + g3, g0 - g3, g1 + g2, g1 - g2
    h1 = root5 * o1
    s03 = o0 - 5.0 * h1
    d03 = e0 + 5.0 * e1
    s12 = o0 + h1
    d12 = root5 * (e0 - e1)
    return s03 - d03, s12 + d12, s12 - d12, s03 + d03


def face_planes():
    odd = lax.rem(lax.axis_index("azim"), 2)
    return 3 * odd, 3 - 3 * odd


def extract_kernel(u, vel, cross, chip, vel_out, sems):
    fields = u.shape[0]
    sides = list(zip((cross, chip), face_planes()))
    copies = [(vel, vel_out)]
    copies += [(vel.at[0, plane], dst.at[fields]) for dst, plane in sides]
    copies = [pltpu.make_async_copy(s, d, sems.at[i]) for i, (s, d) in enumerate(copies)]
    for c in copies:
        c.start()

    def field(f, carry):
        for dst, plane in sides:
            values = [u[f, plane, k] for k in range(16)]
            for k in range(16):
                dst[f, k] = values[k]
        return carry

    lax.fori_loop(0, fields, field, 0)
    for c in copies:
        c.wait()


def extract(u, vel):
    fields = u.shape[0]
    return pl.pallas_call(
        extract_kernel,
        out_shape=[arr(fields + 1, 16, 8, 128)] * 2 + [arr(*vel.shape)],
        in_specs=[vmem, anywhere],
        out_specs=[vmem] * 3,
        scratch_shapes=[pltpu.SemaphoreType.DMA((3,))],
        compiler_params=params(),
    )(u, vel)


def axial_odd():
    return lax.rem(lax.axis_index("axial"), 2) == 1


def rows_kernel(u, vel, send_a, send_b):
    fields = u.shape[0]
    odd = axial_odd()

    def put(f, a, low, high):
        for r in range(4):
            k = a * 4 + r
            send_a[f, k : k + 1, :] = jnp.where(odd, low[r], high[r])
            send_b[f, k : k + 1, :] = jnp.where(odd, high[r], low[r])

    def field(f, carry):
        for a in range(4):
            put(
                f,
                a,
                [u[f, a, r, 0:1, :] for r in range(4)],
                [u[f, a, 12 + r, 7:8, :] for r in range(4)],
            )
        return carry

    lax.fori_loop(0, fields, field, 0)
    for a in range(4):
        put(
            fields,
            a,
            [vel[1, a, r, 0:1, :] * speed_scales[1] for r in range(4)],
            [vel[1, a, 12 + r, 7:8, :] * speed_scales[1] for r in range(4)],
        )


def rows(u, vel):
    fields = u.shape[0]
    return pl.pallas_call(
        rows_kernel,
        out_shape=[arr(fields + 1, 16, 128)] * 2,
        in_specs=[vmem] * 2,
        out_specs=[vmem] * 2,
        compiler_params=params(),
    )(u, vel)


def prepare_kernel(tags, vel, va, cax, crad):
    lane = lax.broadcasted_iota(jnp.int32, tile, 1)
    sub = lax.broadcasted_iota(jnp.int32, tile, 0)
    tag = tags[...]
    inner, outer = lane == 0, lane == 127

    def plane(a, carry):
        for d in range(3):
            for k in range(16):
                va[d, a, k] = vel[d, a, k] * speed_scales[d]
        for r in range(4):
            a0, a3 = va[1, a, r], va[1, a, 12 + r]
            below, above = pltpu.roll(a3, 1, 0), pltpu.roll(a0, 7, 0)
            m_low = jnp.maximum(jnp.abs(a0), jnp.abs(below))
            m_up = jnp.maximum(jnp.abs(a3), jnp.abs(above))
            cax[a, r, 0] = jnp.where(sub == 0, 0.0, -12.0 * m_low)
            cax[a, r, 1] = jnp.where(sub == 0, 0.0, 12.0 * (m_low + below))
            cax[a, r, 2] = jnp.where(sub == 7, 0.0, -12.0 * m_up)
            cax[a, r, 3] = jnp.where(sub == 7, 0.0, 12.0 * (m_up - above))
        for x in range(4):
            a0, a3 = va[2, a, 4 * x], va[2, a, 4 * x + 3]
            below = jnp.where(inner, a0, pltpu.roll(a3, 1, 1))
            above = jnp.where(outer, a3, pltpu.roll(a0, 127, 1))
            m_low = jnp.maximum(jnp.abs(a0), jnp.abs(below))
            m_up = jnp.maximum(jnp.abs(a3), jnp.abs(above))
            own_low, out_low = -12.0 * m_low, 12.0 * (m_low + below)
            own_up, out_up = -12.0 * m_up, 12.0 * (m_up - above)
            own_low = jnp.where(inner & (tag == 0), -12.0 * a0, own_low)
            own_low = jnp.where(inner & (tag == 2), 12.0 * a0, own_low)
            own_up = jnp.where(outer & (tag == 0), 12.0 * a3, own_up)
            own_up = jnp.where(outer & (tag == 2), -12.0 * a3, own_up)
            crad[a, x, 0] = own_low
            crad[a, x, 1] = jnp.where(inner & (tag != 1), 0.0, out_low)
            crad[a, x, 2] = own_up
            crad[a, x, 3] = jnp.where(outer & (tag != 1), 0.0, out_up)
        return carry

    lax.fori_loop(0, 4, plane, 0)


def prepare(tags, vel):
    return pl.pallas_call(
        prepare_kernel,
        out_shape=[arr(3, 4, 16, 8, 128), arr(4, 4, 4, 8, 128), arr(4, 4, 4, 8, 128)],
        in_specs=[vmem] * 2,
        out_specs=[vmem] * 3,
        compiler_params=params(),
    )(tags, vel)


def plane_terms(f, a, keep, src, va, cax, crad, edge):
    lane = lax.broadcasted_iota(jnp.int32, tile, 1)
    u = [src[f, a, k] for k in range(16)]
    acc = [keep * v for v in u]
    for r in range(4):
        line = [u[4 * x + r] for x in range(4)]
        out = volume(*[va[1, a, 4 * x + r] * line[x] for x in range(4)])
        below, above = pltpu.roll(line[3], 1, 0), pltpu.roll(line[0], 7, 0)
        acc[r] += out[0] + (cax[a, r, 0] * line[0] + cax[a, r, 1] * below)
        acc[4 + r] += out[1]
        acc[8 + r] += out[2]
        acc[12 + r] += out[3] + (cax[a, r, 2] * line[3] + cax[a, r, 3] * above)
    for x in range(4):
        line = [u[4 * x + r] for r in range(4)]
        out = volume(*[va[2, a, 4 * x + r] * line[r] for r in range(4)])
        imposed = edge[f, a * 4 + x]
        below = jnp.where(lane == 0, imposed, pltpu.roll(line[3], 1, 1))
        above = jnp.where(lane == 127, imposed, pltpu.roll(line[0], 127, 1))
        acc[4 * x] += out[0] + (crad[a, x, 0] * line[0] + crad[a, x, 1] * below)
        acc[4 * x + 1] += out[1]
        acc[4 * x + 2] += out[2]
        acc[4 * x + 3] += out[3] + (crad[a, x, 2] * line[3] + crad[a, x, 3] * above)
    return acc


def first_kernel(decay, edge, u, va, cax, crad, acc):
    fields = u.shape[0]

    def field(f, carry):
        keep = 1.0 - time_step * decay[f]
        for q in range(4):
            outs = []
            for k in range(4 * q, 4 * q + 4):
                outs.append(volume(*[va[0, a, k] * u[f, a, k] for a in range(4)]))
            for r in range(4):
                for a in range(4):
                    acc[f, a, 4 * q + r] = outs[r][a]
        for a in range(4):
            out = plane_terms(f, a, keep, u, va, cax, crad, edge)
            for k in range(16):
                acc[f, a, k] += out[k]
        return carry

    lax.fori_loop(0, fields, field, 0)


def first_section(decay, edge, u, va, cax, crad):
    fields = u.shape[0]
    return pl.pallas_call(
        first_kernel,
        out_shape=arr(fields, 4, 16, 8, 128),
        in_specs=[smem] + [vmem] * 5,
        out_specs=vmem,
        compiler_params=params(),
    )(decay, edge, u, va, cax, crad)


def second_kernel(decay, edge, u, s1, va, cax, crad, caz, part):
    fields = u.shape[0]

    def field(f, carry):
        keep = 1.0 - time_step * decay[f]
        for q in range(4):
            outs = []
            for k in range(4 * q, 4 * q + 4):
                line = [s1[f, a, k] for a in range(4)]
                out = list(volume(*[va[0, a, k] * line[a] for a in range(4)]))
                out[0] += caz[0, k] * line[0]
                out[3] += caz[3, k] * line[3]
                outs.append(out)
            for r in range(4):
                for a in range(4):
                    part[f, a, 4 * q + r] = outs[r][a]
        for a in range(4):
            out = plane_terms(f, a, keep, s1, va, cax, crad, edge)
            for k in range(16):
                part[f, a, k] = 0.5 * (u[f, a, k] + (part[f, a, k] + out[k]))
        return carry

    lax.fori_loop(0, fields, field, 0)


def second_section(decay, edge, u, s1, va, cax, crad, caz):
    fields = u.shape[0]
    return pl.pallas_call(
        second_kernel,
        out_shape=arr(fields, 4, 16, 8, 128),
        in_specs=[smem] + [vmem] * 7,
        out_specs=vmem,
        compiler_params=params(),
    )(decay, edge, u, s1, va, cax, crad, caz)


def edge_terms(inlet, own_a, own_b, recv_a, recv_b, factors, low, high):
    position = lax.axis_index("axial")
    odd = axial_odd()
    fields = inlet.shape[0]
    own_low = jnp.where(odd, own_a[...], own_b[...])
    own_high = jnp.where(odd, own_b[...], own_a[...])
    below = jnp.where(odd, recv_a[...], recv_b[...])
    above = jnp.where(odd, recv_b[...], recv_a[...])
    if own_a.shape[0] > fields:
        a0, a3 = own_low[fields], own_high[fields]
        a_below = jnp.where(position == 0, a0, below[fields])
        a_above = above[fields]
        is_last = position == lax.axis_size("axial") - 1
        m_low = jnp.maximum(jnp.abs(a0), jnp.abs(a_below))
        m_up = jnp.maximum(jnp.abs(a3), jnp.abs(a_above))
        factors[0] = -12.0 * m_low
        factors[1] = 12.0 * (m_low + a_below)
        factors[2] = jnp.where(is_last, -12.0 * a3, -12.0 * m_up)
        factors[3] = jnp.where(is_last, 0.0, 12.0 * (m_up - a_above))
    from_below = jnp.where(position == 0, inlet[...], below[:fields])
    low[...] = factors[0] * own_low[:fields] + factors[1] * from_below
    high[...] = factors[2] * own_high[:fields] + factors[3] * above[:fields]
    if own_a.shape[0] == fields:
        low[...] = 0.5 * low[...]
        high[...] = 0.5 * high[...]


def close_kernel(
    inlet, own_a, own_b, recv_a, recv_b, recv_x, recv_c, u, va, acc,
    s1, send_x, send_c, caz, low, high, factors,
):
    fields = u.shape[0]
    sub = lax.broadcasted_iota(jnp.int32, tile, 0)
    planes = face_planes()
    edge_terms(inlet, own_a, own_b, recv_a, recv_b, factors, low, high)
    for side, recv in enumerate((recv_x, recv_c)):
        plane = planes[side]
        sign = jnp.where(plane == 0, 1.0, -1.0)
        beside = plane + 1 - lax.div(plane, 3) * 2
        for k in range(16):
            own, other = va[0, plane, k], recv[fields, k] * speed_scales[0]
            m = jnp.maximum(jnp.abs(own), jnp.abs(other))
            caz[plane, k] = -12.0 * m
            caz[beside, k] = 12.0 * (m + sign * other)

    def field(f, carry):
        for side, (recv, send) in enumerate(((recv_x, send_x), (recv_c, send_c))):
            plane = planes[side]
            beside = plane + 1 - lax.div(plane, 3) * 2
            values = []
            for k in range(16):
                value = acc[f, plane, k] + (
                    caz[plane, k] * u[f, plane, k] + caz[beside, k] * recv[f, k]
                )
                if k < 4:
                    row = low[f, pl.ds(plane * 4 + k, 1), :]
                    value += jnp.where(sub == 0, row, 0.0)
                if k >= 12:
                    row = high[f, pl.ds(plane * 4 + k - 12, 1), :]
                    value += jnp.where(sub == 7, row, 0.0)
                values.append(value)
            for k in range(16):
                s1[f, plane, k] = values[k]
                send[f, k] = values[k]
        return carry

    lax.fori_loop(0, fields, field, 0)


def close_first(inlet, own_a, own_b, recv_a, recv_b, recv_x, recv_c, u, va, acc):
    fields = u.shape[0]
    return pl.pallas_call(
        close_kernel,
        out_shape=[
            arr(fields, 4, 16, 8, 128),
            arr(fields, 16, 8, 128),
            arr(fields, 16, 8, 128),
            arr(4, 16, 8, 128),
            arr(fields, 16, 128),
            arr(fields, 16, 128),
            arr(4, 16, 128),
        ],
        in_specs=[vmem] * 10,
        out_specs=[vmem] * 7,
        input_output_aliases={9: 0},
        compiler_params=params(),
    )(inlet, own_a, own_b, recv_a, recv_b, recv_x, recv_c, u, va, acc)


def middle_kernel(low, high, s1_in, s1, send_a, send_b):
    fields = s1.shape[0]
    odd = axial_odd()

    def field(f, carry):
        for a in range(4):
            for r in range(4):
                k = a * 4 + r
                first = s1_in[f, a, r, 0:1, :]
                last = s1_in[f, a, 12 + r, 7:8, :]
                if a in (1, 2):
                    first += low[f, k : k + 1, :]
                    last += high[f, k : k + 1, :]
                    s1[f, a, r, 0:1, :] = first
                    s1[f, a, 12 + r, 7:8, :] = last
                send_a[f, k : k + 1, :] = jnp.where(odd, first, last)
                send_b[f, k : k + 1, :] = jnp.where(odd, last, first)
        return carry

    lax.fori_loop(0, fields, field, 0)


def middle(low, high, s1):
    fields = s1.shape[0]
    return pl.pallas_call(
        middle_kernel,
        out_shape=[arr(*s1.shape), arr(fields, 16, 128), arr(fields, 16, 128)],
        in_specs=[vmem] * 3,
        out_specs=[vmem] * 3,
        input_output_aliases={2: 0},
        compiler_params=params(),
    )(low, high, s1)


def finish_kernel(
    inlet, own_a, own_b, recv_a, recv_b, factors, recv_x, recv_c, caz, part,
    out, low, high, work, sems,
):
    fields = part.shape[0]
    sub = lax.broadcasted_iota(jnp.int32, tile, 0)
    planes = face_planes()
    edge_terms(inlet, own_a, own_b, recv_a, recv_b, factors, low, high)

    def field(f, carry):
        def edged(a, k, value):
            if k < 4:
                row = low[f, pl.ds(a * 4 + k, 1), :]
                return value + jnp.where(sub == 0, row, 0.0)
            if k >= 12:
                row = high[f, pl.ds(a * 4 + k - 12, 1), :]
                return value + jnp.where(sub == 7, row, 0.0)
            return value

        for side, recv in enumerate((recv_x, recv_c)):
            plane = planes[side]
            beside = plane + 1 - lax.div(plane, 3) * 2
            values = []
            for k in range(16):
                value = part[f, plane, k] + 0.5 * (caz[beside, k] * recv[f, k])
                values.append(edged(plane, k, value))
            for k in range(16):
                work[f, plane, k] = values[k]
        for a in (1, 2):
            values = [edged(a, k, part[f, a, k]) for k in range(16)]
            for k in range(16):
                work[f, a, k] = values[k]
        pltpu.make_async_copy(work.at[f], out.at[f], sems.at[f]).start()
        return carry

    lax.fori_loop(0, fields, field, 0)

    def drain(f, carry):
        pltpu.make_async_copy(work.at[f], out.at[f], sems.at[f]).wait()
        return carry

    lax.fori_loop(0, fields, drain, 0)


def finish(inlet, own_a, own_b, recv_a, recv_b, factors, recv_x, recv_c, caz, part):
    fields = part.shape[0]
    return pl.pallas_call(
        finish_kernel,
        out_shape=arr(*part.shape),
        in_specs=[vmem] * 10,
        out_specs=in_hbm,
        scratch_shapes=[
            pltpu.VMEM((fields, 16, 128), jnp.float32),
            pltpu.VMEM((fields, 16, 128), jnp.float32),
            pltpu.VMEM(part.shape, jnp.float32),
            pltpu.SemaphoreType.DMA((fields,)),
        ],
        compiler_params=params(),
    )(inlet, own_a, own_b, recv_a, recv_b, factors, recv_x, recv_c, caz, part)


def swap(array, axis, odd_up):
    count = lax.axis_size(axis)
    if odd_up:
        route = [(i, (i + 1) % count if i % 2 else (i - 1) % count) for i in range(count)]
    else:
        route = [(i, i ^ 1) for i in range(count)]
    return lax.ppermute(array, axis, route)


def per_device(flow_state, velocity, inlet_state, radial_inflow, face_tags, decay_rates):
    fields = flow_state.shape[0]
    u = flow_state.reshape((fields, 4, 16) + tile)
    vel = velocity.reshape((3, 4, 16) + tile)
    inlet = inlet_state.reshape(fields, 16, 128)
    lane = lax.broadcasted_iota(jnp.int32, tile, 1)
    tags = jnp.where(lane == 0, face_tags[0].reshape(8, 1), face_tags[1].reshape(8, 1))
    edges = radial_inflow.reshape(2, fields, 16, 8, 1)
    edge = jnp.where(lane == 0, edges[0], edges[1])

    send_x, send_c, vel = extract(u, vel)
    recv_x = swap(send_x, "azim", True)
    recv_c = swap(send_c, "azim", False)
    u_held, _, _ = lax.optimization_barrier((u, send_x, send_c))
    own_a, own_b = rows(u_held, vel)
    recv_a = swap(own_a, "axial", False)
    recv_b = swap(own_b, "axial", True)

    va, cax, crad = prepare(tags, vel)
    acc = first_section(decay_rates, edge, u, va, cax, crad)
    s1, send_x, send_c, caz, low, high, factors = close_first(
        inlet, own_a, own_b, recv_a, recv_b, recv_x, recv_c, u, va, acc
    )
    recv_x = swap(send_x, "azim", True)
    recv_c = swap(send_c, "azim", False)
    s1, own_a, own_b = middle(low, high, s1)
    recv_a = swap(own_a, "axial", False)
    recv_b = swap(own_b, "axial", True)

    part = second_section(decay_rates, edge, u, s1, va, cax, crad, caz)
    out = finish(inlet, own_a, own_b, recv_a, recv_b, factors, recv_x, recv_c, caz, part)
    return out.reshape(flow_state.shape)


def solution(mesh):
    in_specs = (
        P(None, None, None, None, "azim", "axial", None),
        P(None, None, None, None, "azim", "axial", None),
        P(None, None, None, "azim", None),
        P(None, None, None, None, "azim", "axial"),
        P(None, "azim", "axial"),
        P(),
    )
    out_specs = P(None, None, None, None, "azim", "axial", None)
    return jax.shard_map(
        per_device, mesh=mesh, in_specs=in_specs, out_specs=out_specs, check_vma=False
    )
```

time: 53.2 us -> 48.5 us (0.912)
  Pallas kernels: 16.2 us -> 13.2 us
  other arithmetic: 2.85 us -> 0.52 us
  local copies, waits for them, and re-layouts: 2.64 us -> 4.47 us
  starting transfers between devices: 16.7 us -> 15.3 us
    unnamed x14 -> x18, local copies, waits for them, and re-layouts: 1.16 us -> 4.11 us
    select_n x2 -> x0, other arithmetic: 2.34 us -> none  [the longest x1 1.6 us: per_device(): send_b = jnp.where(odd, high, low)]
    pallas_call x1, Pallas kernels: 5.44 us -> 3.61 us  [second_section(): pl.pallas_call(second_kernel, out_shape=arr(fields, 4, 16, 8, 128), in_sp...]
    ppermute x8, starting transfers between devices: 16.7 us -> 15.3 us  [swap(): return lax.ppermute(array, axis, route)]
    pallas_call x1 -> x4, Pallas kernels: 5.53 us -> 4.21 us  [the longest x1 3.32 us: first_section(): pl.pallas_call(first_kernel, out_shape=arr(fields, 4, 16, 8, 128), in_spe...]
    squeeze x1 -> x0, local copies, waits for them, and re-layouts: 1.12 us -> none  [per_device(): velocity[1:2, :, :, :, 0]]
  transfers between devices with their start and end apart: 8 -> 8, of which waited for: 3 -> 5; matrix products, arithmetic and copies ran while one was open for 2% -> 2% of each run, Pallas kernels for 23% -> 16%
where the time goes in v1:
time: 48.5 us; the launch traced here: 48.2 us
  starting transfers between devices  15.3 us (32%)
  waiting for transfers between devices  14.6 us (30%)
  Pallas kernels  13.2 us (27%)
  local copies, waits for them, and re-layouts  4.47 us (9%)
  other arithmetic  0.52 us (1%)
    ppermute x8, starting transfers between devices, swap(): return lax.ppermute(array, axis, route)  15.3 us
    ppermute x8, waiting for transfers between devices, swap(): return lax.ppermute(array, axis, route)  14.6 us
    unnamed x18, local copies, waits for them, and re-layouts  4.11 us
    pallas_call x1, Pallas kernels, second_section(): pl.pallas_call(second_kernel, out_shape=arr(fields, 4, 16, 8, 128), in_sp...  3.61 us
    pallas_call x1, Pallas kernels, first_section(): pl.pallas_call(first_kernel, out_shape=arr(fields, 4, 16, 8, 128), in_spe...  3.32 us
    pallas_call x1, Pallas kernels, close_first(): pl.pallas_call(close_kernel, out_shape=[arr(fields, 4, 16, 8, 128), arr(f...  2.07 us
    pallas_call x1, Pallas kernels, finish(): pl.pallas_call(finish_kernel, out_shape=arr(*part.shape), in_specs=[vmem]...  1.79 us
    pallas_call x1, Pallas kernels, extract(): pl.pallas_call(extract_kernel, out_shape=[arr(fields + 1, 16, 8, 128)] *...  1.51 us
  transfers between devices with their start and end apart: 8, of which 5 were waited for; matrix products, arithmetic and copies ran while one was open for 2% of the time, Pallas kernels for 16%

profile of v1, /device:TPU:0, one launch (start us, length us, event | category | flops | bytes accessed | tf_op | source)
XLA Modules:
  0.0 48.2 jit_solution(8112880066635276282)
XLA Ops:
  0.0 0.0 copy-start
  0.0 1.8 %copy-done = f32[11,4,4,4,1,8,128]{6,5,4,3,2,1,0:T(8,128)S(1)} copy-done((f32[11,4,4,4,1,8,128]{6,5,4,3,2,1,0:T(8,128)S(1)}, f32[11,4,4,4,1,8,128]{6,5,4,3,2,1,0:T(8,128)}, u32[]{:S(2)}) %copy-start) | copy-done | bytes 2883608
  1.8 0.0 copy-start.4
  1.8 1.1 %copy-done.4 = f32[3,4,4,4,1,8,128]{6,5,4,3,2,1,0:T(8,128)S(1)} copy-done((f32[3,4,4,4,1,8,128]{6,5,4,3,2,1,0:T(8,128)S(1)}, f32[3,4,4,4,1,8,128]{6,5,4,3,2,1,0:T(8,128)}, u32[]{:S(2)}) %copy-start.4) | copy-done | bytes 786456
  2.9 0.0 copy-start.7
  3.0 1.5 %shard_map.64 = (f32[12,16,8,128]{3,2,1,0:T(8,128)}, f32[12,16,8,128]{3,2,1,0:T(8,128)}, f32[3,4,16,8,128]{4,3,2,1,0:T(8,128)S(1)}) custom-call(f32[11,4,16,8,128]{4,3,2,1,0:T(8,128)S(1)} %bitcast.12, f32[3,4,16,8,128]{4,3,2,1,0:T(8,128)S(1)} %bitcast.17), custom_call_target="tpu_custom_call" | custom-call | tf_op jit(solution)/shard_map/pallas_call | solution.py:67
  4.5 0.0 copy-start.2
  4.5 0.0 copy-start.8
  4.5 6.1 %collective-permute-start.2 = (f32[12,16,8,128]{3,2,1,0:T(8,128)}, f32[12,16,8,128]{3,2,1,0:T(8,128)}, u32[]{:S(2)}, u32[]{:S(2)}) collective-permute-start(f32[12,16,8,128]{3,2,1,0:T(8,128)} %get-tuple-element.24), channel_id=1, source_target_pairs={{0,120},{8,16},{16,8},{24,32},{32,24},{40,48},{48,40},{56,64},{64,... | collective-permute-start | bytes 2359304 | tf_op jit(solution)/shard_map/ppermute | solution.py:455
  10.6 0.0 collective-permute-start.3
  10.6 0.0 copy-start.1
  10.6 0.0 copy-start.6
  10.6 0.2 shard_map.65
  10.8 0.0 copy-done.2
  10.8 0.7 %collective-permute-start = (f32[12,16,128]{2,1,0:T(8,128)S(1)}, f32[12,16,128]{2,1,0:T(8,128)S(1)}, u32[]{:S(2)}, u32[]{:S(2)}) collective-permute-start(f32[12,16,128]{2,1,0:T(8,128)S(1)} %get-tuple-element.28.own_a), channel_id=1, source_target_pairs={{0,1},{1,0},{2,3},{3,2},{4,5},{5,4},{6,7},{7,6},{8,9},{9,8},{10,11... | collective-permute-start | bytes 294920 | tf_op jit(solution)/shard_map/ppermute | solution.py:455
  11.5 3.9 %collective-permute-start.1 = (f32[12,16,128]{2,1,0:T(8,128)S(1)}, f32[12,16,128]{2,1,0:T(8,128)S(1)}, u32[]{:S(2)}, u32[]{:S(2)}) collective-permute-start(f32[12,16,128]{2,1,0:T(8,128)S(1)} %get-tuple-element.29.own_b), channel_id=1, source_target_pairs={{0,7},{1,2},{2,1},{3,4},{4,3},{5,6},{6,5},{7,0},{8,15},{9,10},{10,... | collective-permute-start | bytes 294920 | tf_op jit(solution)/shard_map/ppermute | solution.py:455
  15.4 0.0 copy-done.7
  15.4 0.2 copy.10
  15.6 0.2 copy.9
  15.7 0.0 copy-done.8
  15.8 0.4 broadcast_select_fusion.edge
  16.2 0.1 broadcast_select_fusion.1.tags
  16.3 0.0 copy-start.3
  16.3 1.1 %copy-done.3 = f32[3,4,16,8,128]{4,3,2,1,0:T(8,128)S(1)} copy-done((f32[3,4,16,8,128]{4,3,2,1,0:T(8,128)S(1)}, f32[3,4,16,8,128]{4,3,2,1,0:T(8,128)}, u32[]{:S(2)}) %copy-start.3) | copy-done | bytes 786456
  17.4 0.4 shard_map.66
  17.8 0.0 copy-done.1
  17.8 0.0 copy-done.6
  17.8 0.0 copy-start.5
  17.8 3.3 %shard_map.67.acc = f32[11,4,16,8,128]{4,3,2,1,0:T(8,128)S(1)} custom-call(f32[11]{0:T(128)S(1)} %copy-done.6, f32[11,16,8,128]{3,2,1,0:T(8,128)S(1)} %broadcast_select_fusion.edge, f32[11,4,16,8,128]{4,3,2,1,0:T(8,128)S(1)} %bitcast.14, f32[3,4,16,8,128]{4,3,2,1,0:T(8,128)S(1)} %get-tuple-element.30.va, f32[4,4,4,8,128]{4,3,2,1,0:T(8,128)S(1)} %get-tuple-element.31.cax, ...), custom_call_target="tpu_custom_call" | custom-call | tf_op jit(solution)/shard_map/pallas_call | solution.py:220
  21.1 3.4 %collective-permute-done.recv_a = f32[12,16,128]{2,1,0:T(8,128)S(1)} collective-permute-done((f32[12,16,128]{2,1,0:T(8,128)S(1)}, f32[12,16,128]{2,1,0:T(8,128)S(1)}, u32[]{:S(2)}, u32[]{:S(2)}) %collective-permute-start) | collective-permute-done | bytes 98336 | tf_op jit(solution)/shard_map/ppermute | solution.py:455
  24.5 3.5 %collective-permute-done.1.recv_b = f32[12,16,128]{2,1,0:T(8,128)S(1)} collective-permute-done((f32[12,16,128]{2,1,0:T(8,128)S(1)}, f32[12,16,128]{2,1,0:T(8,128)S(1)}, u32[]{:S(2)}, u32[]{:S(2)}) %collective-permute-start.1) | collective-permute-done | bytes 98336 | tf_op jit(solution)/shard_map/ppermute | solution.py:455
  28.0 0.0 collective-permute-done.2.recv_x
  28.0 0.0 collective-permute-done.3.recv_c
  28.0 0.0 copy-done.5
  28.0 2.1 %shard_map.68 = (f32[11,4,16,8,128]{4,3,2,1,0:T(8,128)S(1)}, f32[11,16,8,128]{3,2,1,0:T(8,128)S(1)}, f32[11,16,8,128]{3,2,1,0:T(8,128)S(1)}, f32[4,16,8,128]{3,2...) custom-call(f32[11,16,128]{2,1,0:T(8,128)S(1)} %bitcast.18, ...), custom_call_target="tpu_custom_call", output_to_operand_aliasing={{0}: (9, {})} | custom-call | tf_op jit(solution)/shard_map/pallas_call | solution.py:336
  30.1 0.1 collective-permute-start.6
  30.2 0.0 collective-permute-start.7
  30.3 0.3 shard_map.69
  30.6 0.6 %collective-permute-start.4 = (f32[11,16,128]{2,1,0:T(8,128)S(1)}, f32[11,16,128]{2,1,0:T(8,128)S(1)}, u32[]{:S(2)}, u32[]{:S(2)}) collective-permute-start(f32[11,16,128]{2,1,0:T(8,128)S(1)} %get-tuple-element.36.own_a), channel_id=1, source_target_pairs={{0,1},{1,0},{2,3},{3,2},{4,5},{5,4},{6,7},{7,6},{8,9},{9,8},{10,11... | collective-permute-start | bytes 270344 | tf_op jit(solution)/shard_map/ppermute | solution.py:455
  31.2 3.9 %collective-permute-start.5 = (f32[11,16,128]{2,1,0:T(8,128)S(1)}, f32[11,16,128]{2,1,0:T(8,128)S(1)}, u32[]{:S(2)}, u32[]{:S(2)}) collective-permute-start(f32[11,16,128]{2,1,0:T(8,128)S(1)} %get-tuple-element.37.own_b), channel_id=1, source_target_pairs={{0,7},{1,2},{2,1},{3,4},{4,3},{5,6},{6,5},{7,0},{8,15},{9,10},{10,... | collective-permute-start | bytes 270344 | tf_op jit(solution)/shard_map/ppermute | solution.py:455
  35.1 3.6 %shard_map.70.part = f32[11,4,16,8,128]{4,3,2,1,0:T(8,128)S(1)} custom-call(f32[11]{0:T(128)S(1)} %copy-done.6, f32[11,16,8,128]{3,2,1,0:T(8,128)S(1)} %broadcast_select_fusion.edge, f32[11,4,16,8,128]{4,3,2,1,0:T(8,128)S(1)} %bitcast.16, f32[11,4,16,8,128]{4,3,2,1,0:T(8,128)S(1)} %get-tuple-element.42.s1, f32[3,4,16,8,128]{4,3,2,1,0:T(8,128)S(1)} %get-tuple-element.30.va, ...), custom_call_target="tpu_custom_call" | custom-call | tf_op jit(solution)/shard_map/pallas_call | solution.py:256
  38.7 4.3 %collective-permute-done.4.recv_a = f32[11,16,128]{2,1,0:T(8,128)S(1)} collective-permute-done((f32[11,16,128]{2,1,0:T(8,128)S(1)}, f32[11,16,128]{2,1,0:T(8,128)S(1)}, u32[]{:S(2)}, u32[]{:S(2)}) %collective-permute-start.4) | collective-permute-done | bytes 90144 | tf_op jit(solution)/shard_map/ppermute | solution.py:455
  42.9 3.4 %collective-permute-done.5.recv_b = f32[11,16,128]{2,1,0:T(8,128)S(1)} collective-permute-done((f32[11,16,128]{2,1,0:T(8,128)S(1)}, f32[11,16,128]{2,1,0:T(8,128)S(1)}, u32[]{:S(2)}, u32[]{:S(2)}) %collective-permute-start.5) | collective-permute-done | bytes 90144 | tf_op jit(solution)/shard_map/ppermute | solution.py:455
  46.4 0.1 collective-permute-done.6.recv_x
  46.4 0.0 collective-permute-done.7.recv_c
  46.5 1.8 %shard_map.71 = f32[11,4,16,8,128]{4,3,2,1,0:T(8,128)} custom-call(f32[11,16,128]{2,1,0:T(8,128)S(1)} %bitcast.19, f32[11,16,128]{2,1,0:T(8,128)S(1)} %get-tuple-element.36.own_a, f32[11,16,128]{2,1,0:T(8,128)S(1)} %get-tuple-element.37.own_b, f32[11,16,128]{2,1,0:T(8,128)S(1)} %collective-permute-done.4.recv_a, ...), custom_call_target="tpu_custom_call" | custom-call | tf_op jit(solution)/shard_map/pallas_call | solution.py:434
  (3 shorter events, 0.0 us)
Async XLA Ops:
  0.0 1.8 %copy-start = (f32[11,4,4,4,1,8,128]{6,5,4,3,2,1,0:T(8,128)S(1)}, f32[11,4,4,4,1,8,128]{6,5,4,3,2,1,0:T(8,128)}, u32[]{:S(2)}) copy-start(f32[11,4,4,4,1,8,128]{6,5,4,3,2,1,0:T(8,128)} %param.6) | copy-start | bytes 8650756
  1.8 1.1 %copy-start.4 = (f32[3,4,4,4,1,8,128]{6,5,4,3,2,1,0:T(8,128)S(1)}, f32[3,4,4,4,1,8,128]{6,5,4,3,2,1,0:T(8,128)}, u32[]{:S(2)}) copy-start(f32[3,4,4,4,1,8,128]{6,5,4,3,2,1,0:T(8,128)} %param.7) | copy-start | bytes 2359300
  2.9 12.4 %copy-start.7 = (f32[2,11,4,4,1,8]{1,5,4,3,2,0:T(8,128)S(1)}, f32[2,11,4,4,1,8]{1,5,4,3,2,0:T(8,128)}, u32[]{:S(2)}) copy-start(f32[2,11,4,4,1,8]{1,5,4,3,2,0:T(8,128)} %param.9) | copy-start | bytes 33796
  4.5 6.3 %copy-start.2 = (f32[3,4,16,8,128]{4,3,2,1,0:T(8,128)}, f32[3,4,16,8,128]{4,3,2,1,0:T(8,128)S(1)}, u32[]{:S(2)}) copy-start(f32[3,4,16,8,128]{4,3,2,1,0:T(8,128)S(1)} %get-tuple-element.27.vel) | copy-start | bytes 2359300
  4.5 11.3 %copy-start.8 = (s32[2,1,8]{2,1,0:T(1,128)S(1)}, s32[2,1,8]{2,1,0:T(1,128)}, u32[]{:S(2)}) copy-start(s32[2,1,8]{2,1,0:T(1,128)} %param.10) | copy-start | bytes 196
  4.5 23.5 %collective-permute-start.2 = (f32[12,16,8,128]{3,2,1,0:T(8,128)}, f32[12,16,8,128]{3,2,1,0:T(8,128)}, u32[]{:S(2)}, u32[]{:S(2)}) collective-permute-start(f32[12,16,8,128]{3,2,1,0:T(8,128)} %get-tuple-element.24), channel_id=1, source_target_pairs={{0,120},{8,16},{16,8},{24,32},{32,24},{40,48},{48,40},{56,64},{64,... | collective-permute-start | bytes 2359304 | tf_op jit(solution)/shard_map/ppermute | solution.py:455
  10.6 17.4 %collective-permute-start.3 = (f32[12,16,8,128]{3,2,1,0:T(8,128)}, f32[12,16,8,128]{3,2,1,0:T(8,128)}, u32[]{:S(2)}, u32[]{:S(2)}) collective-permute-start(f32[12,16,8,128]{3,2,1,0:T(8,128)} %get-tuple-element.25), channel_id=1, source_target_pairs={{0,8},{8,0},{16,24},{24,16},{32,40},{40,32},{48,56},{56,48},{64,72... | collective-permute-start | bytes 2359304 | tf_op jit(solution)/shard_map/ppermute | solution.py:455
  10.6 7.2 %copy-start.1 = (f32[11,4,4,4,1,8,128]{6,5,4,3,2,1,0:T(8,128)S(1)}, f32[11,4,4,4,1,8,128]{6,5,4,3,2,1,0:T(8,128)}, u32[]{:S(2)}) copy-start(f32[11,4,4,4,1,8,128]{6,5,4,3,2,1,0:T(8,128)} %param.6) | copy-start | bytes 8650756
  10.6 7.2 %copy-start.6 = (f32[11]{0:T(128)S(1)}, f32[11]{0:T(128)}, u32[]{:S(2)}) copy-start(f32[11]{0:T(128)} %decay.3) | copy-start | bytes 136
  10.8 13.7 %collective-permute-start = (f32[12,16,128]{2,1,0:T(8,128)S(1)}, f32[12,16,128]{2,1,0:T(8,128)S(1)}, u32[]{:S(2)}, u32[]{:S(2)}) collective-permute-start(f32[12,16,128]{2,1,0:T(8,128)S(1)} %get-tuple-element.28.own_a), channel_id=1, source_target_pairs={{0,1},{1,0},{2,3},{3,2},{4,5},{5,4},{6,7},{7,6},{8,9},{9,8},{10,11... | collective-permute-start | bytes 294920 | tf_op jit(solution)/shard_map/ppermute | solution.py:455
  11.5 16.5 %collective-permute-start.1 = (f32[12,16,128]{2,1,0:T(8,128)S(1)}, f32[12,16,128]{2,1,0:T(8,128)S(1)}, u32[]{:S(2)}, u32[]{:S(2)}) collective-permute-start(f32[12,16,128]{2,1,0:T(8,128)S(1)} %get-tuple-element.29.own_b), channel_id=1, source_target_pairs={{0,7},{1,2},{2,1},{3,4},{4,3},{5,6},{6,5},{7,0},{8,15},{9,10},{10,... | collective-permute-start | bytes 294920 | tf_op jit(solution)/shard_map/ppermute | solution.py:455
  16.3 1.1 %copy-start.3 = (f32[3,4,16,8,128]{4,3,2,1,0:T(8,128)S(1)}, f32[3,4,16,8,128]{4,3,2,1,0:T(8,128)}, u32[]{:S(2)}) copy-start(f32[3,4,16,8,128]{4,3,2,1,0:T(8,128)} %copy-done.2) | copy-start | bytes 2359300
  17.8 10.2 %copy-start.5 = (f32[11,4,4,1,128]{4,3,2,1,0:T(1,128)S(1)}, f32[11,4,4,1,128]{4,3,2,1,0:T(1,128)}, u32[]{:S(2)}) copy-start(f32[11,4,4,1,128]{4,3,2,1,0:T(1,128)} %param.8) | copy-start | bytes 270340
  30.1 16.3 %collective-permute-start.6 = (f32[11,16,8,128]{3,2,1,0:T(8,128)S(1)}, f32[11,16,8,128]{3,2,1,0:T(8,128)S(1)}, u32[]{:S(2)}, u32[]{:S(2)}) collective-permute-start(f32[11,16,8,128]{3,2,1,0:T(8,128)S(1)} %get-tuple-element.39), channel_id=1, source_target_pairs={{0,120},{8,16},{16,8},{24,32},{32,24},{40,48},{48,40},{56,64},{64,... | collective-permute-start | bytes 2162696 | tf_op jit(solution)/shard_map/ppermute | solution.py:455
  30.2 16.2 %collective-permute-start.7 = (f32[11,16,8,128]{3,2,1,0:T(8,128)S(1)}, f32[11,16,8,128]{3,2,1,0:T(8,128)S(1)}, u32[]{:S(2)}, u32[]{:S(2)}) collective-permute-start(f32[11,16,8,128]{3,2,1,0:T(8,128)S(1)} %get-tuple-element.40), channel_id=1, source_target_pairs={{0,8},{8,0},{16,24},{24,16},{32,40},{40,32},{48,56},{56,48},{64,72... | collective-permute-start | bytes 2162696 | tf_op jit(solution)/shard_map/ppermute | solution.py:455
  30.6 12.3 %collective-permute-start.4 = (f32[11,16,128]{2,1,0:T(8,128)S(1)}, f32[11,16,128]{2,1,0:T(8,128)S(1)}, u32[]{:S(2)}, u32[]{:S(2)}) collective-permute-start(f32[11,16,128]{2,1,0:T(8,128)S(1)} %get-tuple-element.36.own_a), channel_id=1, source_target_pairs={{0,1},{1,0},{2,3},{3,2},{4,5},{5,4},{6,7},{7,6},{8,9},{9,8},{10,11... | collective-permute-start | bytes 270344 | tf_op jit(solution)/shard_map/ppermute | solution.py:455
  31.2 15.2 %collective-permute-start.5 = (f32[11,16,128]{2,1,0:T(8,128)S(1)}, f32[11,16,128]{2,1,0:T(8,128)S(1)}, u32[]{:S(2)}, u32[]{:S(2)}) collective-permute-start(f32[11,16,128]{2,1,0:T(8,128)S(1)} %get-tuple-element.37.own_b), channel_id=1, source_target_pairs={{0,7},{1,2},{2,1},{3,4},{4,3},{5,6},{6,5},{7,0},{8,15},{9,10},{10,... | collective-permute-start | bytes 270344 | tf_op jit(solution)/shard_map/ppermute | solution.py:455

commit v2 on v1

v2 whole, which is shorter than its diff:
```python
import functools

import jax
import jax.numpy as jnp
import numpy as np
from jax import lax
from jax.experimental import pallas as pl
from jax.experimental.pallas import tpu as pltpu
from jax.sharding import PartitionSpec as P

time_step = 0.025
metric_scales = (2.0, 1.6, 2.4)
root5 = float(np.sqrt(5.0))
speed_scales = tuple(0.25 * c * time_step for c in metric_scales)
vmem = pl.BlockSpec(memory_space=pltpu.VMEM)
smem = pl.BlockSpec(memory_space=pltpu.SMEM)
anywhere = pl.BlockSpec(memory_space=pl.ANY)
in_hbm = pl.BlockSpec(memory_space=pltpu.HBM)
vmem_limit = 16 * 1024 * 1024
tile = (8, 128)


def params(limit=vmem_limit):
    return pltpu.CompilerParams(vmem_limit_bytes=limit)


def arr(*shape):
    return jax.ShapeDtypeStruct(shape, jnp.float32)


def volume(g0, g1, g2, g3):
    e0, o0, e1, o1 = g0 + g3, g0 - g3, g1 + g2, g1 - g2
    h1 = root5 * o1
    s03 = o0 - 5.0 * h1
    d03 = e0 + 5.0 * e1
    s12 = o0 + h1
    d12 = root5 * (e0 - e1)
    return s03 - d03, s12 + d12, s12 - d12, s03 + d03


def depart_kernel(u, vel, rows_low, rows_high, face_low, face_high):
    fields = u.shape[0]

    def put(f, a, low, high):
        for r in range(4):
            k = a * 4 + r
            rows_low[f, k : k + 1, :] = low[r]
            rows_high[f, k : k + 1, :] = high[r]

    def field(f, carry):
        for a in range(4):
            put(
                f,
                a,
                [u[f, a, r, 0:1, :] for r in range(4)],
                [u[f, a, 12 + r, 7:8, :] for r in range(4)],
            )
        for dst, plane in ((face_low, 0), (face_high, 3)):
            values = [u[f, plane, k] for k in range(16)]
            for k in range(16):
                dst[f, k] = values[k]
        return carry

    lax.fori_loop(0, fields, field, 0)
    for a in range(4):
        put(
            fields,
            a,
            [vel[1, a, r, 0:1, :] * speed_scales[1] for r in range(4)],
            [vel[1, a, 12 + r, 7:8, :] * speed_scales[1] for r in range(4)],
        )
    for dst, plane in ((face_low, 0), (face_high, 3)):
        values = [vel[0, plane, k] * speed_scales[0] for k in range(16)]
        for k in range(16):
            dst[fields, k] = values[k]


def depart(u, vel):
    fields = u.shape[0]
    return pl.pallas_call(
        depart_kernel,
        out_shape=[arr(fields + 1, 16, 128)] * 2 + [arr(fields + 1, 16, 8, 128)] * 2,
        in_specs=[vmem] * 2,
        out_specs=[vmem] * 4,
        compiler_params=params(),
    )(u, vel)


def prepare_kernel(tags, inflow, vel, va, cax, crad, edge):
    lane = lax.broadcasted_iota(jnp.int32, tile, 1)
    sub = lax.broadcasted_iota(jnp.int32, tile, 0)
    tag = tags[...]
    inner, outer = lane == 0, lane == 127

    def imposed(k, carry):
        within, beyond = inflow[0, k], inflow[1, k]
        for f in range(edge.shape[0]):
            edge[f, k] = jnp.where(inner, within[:, f : f + 1], beyond[:, f : f + 1])
        return carry

    lax.fori_loop(0, 16, imposed, 0)

    def plane(a, carry):
        for d in range(3):
            for k in range(16):
                va[d, a, k] = vel[d, a, k] * speed_scales[d]
        for r in range(4):
            a0, a3 = va[1, a, r], va[1, a, 12 + r]
            below, above = pltpu.roll(a3, 1, 0), pltpu.roll(a0, 7, 0)
            m_low = jnp.maximum(jnp.abs(a0), jnp.abs(below))
            m_up = jnp.maximum(jnp.abs(a3), jnp.abs(above))
            cax[a, r, 0] = jnp.where(sub == 0, 0.0, -12.0 * m_low)
            cax[a, r, 1] = jnp.where(sub == 0, 0.0, 12.0 * (m_low + below))
            cax[a, r, 2] = jnp.where(sub == 7, 0.0, -12.0 * m_up)
            cax[a, r, 3] = jnp.where(sub == 7, 0.0, 12.0 * (m_up - above))
        for x in range(4):
            a0, a3 = va[2, a, 4 * x], va[2, a, 4 * x + 3]
            below = jnp.where(inner, a0, pltpu.roll(a3, 1, 1))
            above = jnp.where(outer, a3, pltpu.roll(a0, 127, 1))
            m_low = jnp.maximum(jnp.abs(a0), jnp.abs(below))
            m_up = jnp.maximum(jnp.abs(a3), jnp.abs(above))
            own_low, out_low = -12.0 * m_low, 12.0 * (m_low + below)
            own_up, out_up = -12.0 * m_up, 12.0 * (m_up - above)
            own_low = jnp.where(inner & (tag == 0), -12.0 * a0, own_low)
            own_low = jnp.where(inner & (tag == 2), 12.0 * a0, own_low)
            own_up = jnp.where(outer & (tag == 0), 12.0 * a3, own_up)
            own_up = jnp.where(outer & (tag == 2), -12.0 * a3, own_up)
            crad[a, x, 0] = own_low
            crad[a, x, 1] = jnp.where(inner & (tag != 1), 0.0, out_low)
            crad[a, x, 2] = own_up
            crad[a, x, 3] = jnp.where(outer & (tag != 1), 0.0, out_up)
        return carry

    lax.fori_loop(0, 4, plane, 0)


def prepare(tags, inflow, vel):
    return pl.pallas_call(
        prepare_kernel,
        out_shape=[
            arr(3, 4, 16, 8, 128),
            arr(4, 4, 4, 8, 128),
            arr(4, 4, 4, 8, 128),
            arr(inflow.shape[-1], 16, 8, 128),
        ],
        in_specs=[vmem] * 3,
        out_specs=[vmem] * 4,
        compiler_params=params(),
    )(tags, inflow, vel)


def plane_terms(f, a, keep, src, va, cax, crad, edge):
    lane = lax.broadcasted_iota(jnp.int32, tile, 1)
    u = [src[f, a, k] for k in range(16)]
    acc = [keep * v for v in u]
    for r in range(4):
        line = [u[4 * x + r] for x in range(4)]
        out = volume(*[va[1, a, 4 * x + r] * line[x] for x in range(4)])
        below, above = pltpu.roll(line[3], 1, 0), pltpu.roll(line[0], 7, 0)
        acc[r] += out[0] + (cax[a, r, 0] * line[0] + cax[a, r, 1] * below)
        acc[4 + r] += out[1]
        acc[8 + r] += out[2]
        acc[12 + r] += out[3] + (cax[a, r, 2] * line[3] + cax[a, r, 3] * above)
    for x in range(4):
        line = [u[4 * x + r] for r in range(4)]
        out = volume(*[va[2, a, 4 * x + r] * line[r] for r in range(4)])
        imposed = edge[f, a * 4 + x]
        below = jnp.where(lane == 0, imposed, pltpu.roll(line[3], 1, 1))
        above = jnp.where(lane == 127, imposed, pltpu.roll(line[0], 127, 1))
        acc[4 * x] += out[0] + (crad[a, x, 0] * line[0] + crad[a, x, 1] * below)
        acc[4 * x + 1] += out[1]
        acc[4 * x + 2] += out[2]
        acc[4 * x + 3] += out[3] + (crad[a, x, 2] * line[3] + crad[a, x, 3] * above)
    return acc


def first_kernel(decay, edge, u, va, cax, crad, acc):
    fields = u.shape[0]

    def field(f, carry):
        keep = 1.0 - time_step * decay[f]
        for q in range(4):
            outs = []
            for k in range(4 * q, 4 * q + 4):
                outs.append(volume(*[va[0, a, k] * u[f, a, k] for a in range(4)]))
            for r in range(4):
                for a in range(4):
                    acc[f, a, 4 * q + r] = outs[r][a]
        for a in range(4):
            out = plane_terms(f, a, keep, u, va, cax, crad, edge)
            for k in range(16):
                acc[f, a, k] += out[k]
        return carry

    lax.fori_loop(0, fields, field, 0)


def first_section(decay, edge, u, va, cax, crad):
    fields = u.shape[0]
    return pl.pallas_call(
        first_kernel,
        out_shape=arr(fields, 4, 16, 8, 128),
        in_specs=[smem] + [vmem] * 5,
        out_specs=vmem,
        compiler_params=params(),
    )(decay, edge, u, va, cax, crad)


def second_kernel(decay, edge, u, s1, va, cax, crad, caz, part):
    fields = u.shape[0]

    def field(f, carry):
        keep = 1.0 - time_step * decay[f]
        for q in range(4):
            outs = []
            for k in range(4 * q, 4 * q + 4):
                line = [s1[f, a, k] for a in range(4)]
                out = list(volume(*[va[0, a, k] * line[a] for a in range(4)]))
                out[0] += caz[0, k] * line[0]
                out[3] += caz[3, k] * line[3]
                outs.append(out)
            for r in range(4):
                for a in range(4):
                    part[f, a, 4 * q + r] = outs[r][a]
        for a in range(4):
            out = plane_terms(f, a, keep, s1, va, cax, crad, edge)
            for k in range(16):
                part[f, a, k] = 0.5 * (u[f, a, k] + (part[f, a, k] + out[k]))
        return carry

    lax.fori_loop(0, fields, field, 0)


def second_section(decay, edge, u, s1, va, cax, crad, caz):
    fields = u.shape[0]
    return pl.pallas_call(
        second_kernel,
        out_shape=arr(fields, 4, 16, 8, 128),
        in_specs=[smem] + [vmem] * 7,
        out_specs=vmem,
        compiler_params=params(),
    )(decay, edge, u, s1, va, cax, crad, caz)


def azim_odd():
    return lax.rem(lax.axis_index("azim"), 2) == 1


def edges_kernel(scale, known, inlet, own_low, own_high, below, above, *refs):
    given, low, high = refs[:-2], refs[-2], refs[-1]
    factors = given[0]
    position = lax.axis_index("axial")
    fields = inlet.shape[0]
    if not known:
        a0, a3 = own_low[fields], own_high[fields]
        a_below = jnp.where(position == 0, a0, below[fields])
        a_above = above[fields]
        is_last = position == lax.axis_size("axial") - 1
        m_low = jnp.maximum(jnp.abs(a0), jnp.abs(a_below))
        m_up = jnp.maximum(jnp.abs(a3), jnp.abs(a_above))
        factors[0] = -12.0 * m_low
        factors[1] = 12.0 * (m_low + a_below)
        factors[2] = jnp.where(is_last, -12.0 * a3, -12.0 * m_up)
        factors[3] = jnp.where(is_last, 0.0, 12.0 * (m_up - a_above))
    for f in range(fields):
        from_below = jnp.where(position == 0, inlet[f], below[f])
        low[f] = scale * (factors[0] * own_low[f] + factors[1] * from_below)
        high[f] = scale * (factors[2] * own_high[f] + factors[3] * above[f])


def edges(scale, inlet, own_low, own_high, below, above, factors=None):
    fields = inlet.shape[0]
    known = factors is not None
    given = [inlet, own_low, own_high, below, above] + ([factors] if known else [])
    out = [arr(fields, 16, 128)] * 2
    if not known:
        out = [arr(4, 16, 128)] + out
    result = pl.pallas_call(
        functools.partial(edges_kernel, scale, known),
        out_shape=out,
        in_specs=[vmem] * len(given),
        out_specs=[vmem] * len(out),
        compiler_params=params(),
    )(*given)
    return ([factors] if known else []) + list(result)


def close_kernel(
    low, high, below, above, u, va, acc, s1, cross, chip, rows_low, rows_high, caz
):
    fields = u.shape[0]
    sub = lax.broadcasted_iota(jnp.int32, tile, 0)
    odd = azim_odd()
    for recv, plane, beside, sign in ((below, 0, 1, 1.0), (above, 3, 2, -1.0)):
        for k in range(16):
            own, other = va[0, plane, k], recv[fields, k]
            m = jnp.maximum(jnp.abs(own), jnp.abs(other))
            caz[plane, k] = -12.0 * m
            caz[beside, k] = 12.0 * (m + sign * other)

    def field(f, carry):
        def row(k, first, last):
            rows_low[f, k : k + 1, :] = first
            rows_high[f, k : k + 1, :] = last

        faces = []
        for recv, plane, beside in ((below, 0, 1), (above, 3, 2)):
            values = []
            for k in range(16):
                value = acc[f, plane, k] + (
                    caz[plane, k] * u[f, plane, k] + caz[beside, k] * recv[f, k]
                )
                if k < 4:
                    term = low[f, pl.ds(plane * 4 + k, 1), :]
                    value += jnp.where(sub == 0, term, 0.0)
                if k >= 12:
                    term = high[f, pl.ds(plane * 4 + k - 12, 1), :]
                    value += jnp.where(sub == 7, term, 0.0)
                values.append(value)
            for k in range(16):
                s1[f, plane, k] = values[k]
            for r in range(4):
                row(plane * 4 + r, values[r][0:1], values[12 + r][7:8])
            faces.append(values)
        for k in range(16):
            cross[f, k] = jnp.where(odd, faces[1][k], faces[0][k])
            chip[f, k] = jnp.where(odd, faces[0][k], faces[1][k])
        for a in (1, 2):
            for r in range(4):
                k = a * 4 + r
                first = acc[f, a, r, 0:1, :] + low[f, k : k + 1, :]
                last = acc[f, a, 12 + r, 7:8, :] + high[f, k : k + 1, :]
                s1[f, a, r, 0:1, :] = first
                s1[f, a, 12 + r, 7:8, :] = last
                row(k, first, last)
        return carry

    lax.fori_loop(0, fields, field, 0)


def close_first(low, high, below, above, u, va, acc):
    fields = u.shape[0]
    return pl.pallas_call(
        close_kernel,
        out_shape=[
            arr(fields, 4, 16, 8, 128),
            arr(fields, 16, 8, 128),
            arr(fields, 16, 8, 128),
            arr(fields, 16, 128),
            arr(fields, 16, 128),
            arr(4, 16, 8, 128),
        ],
        in_specs=[vmem] * 7,
        out_specs=[vmem] * 6,
        input_output_aliases={6: 0},
        compiler_params=params(),
    )(low, high, below, above, u, va, acc)


def finish_kernel(
    low, high, cross, chip, caz, part, out, work, sems
):
    fields = part.shape[0]
    sub = lax.broadcasted_iota(jnp.int32, tile, 0)
    odd = azim_odd()

    def field(f, carry):
        def edged(a, k, value):
            if k < 4:
                row = low[f, pl.ds(a * 4 + k, 1), :]
                return value + jnp.where(sub == 0, row, 0.0)
            if k >= 12:
                row = high[f, pl.ds(a * 4 + k - 12, 1), :]
                return value + jnp.where(sub == 7, row, 0.0)
            return value

        for lower, upper, plane, beside in ((cross, chip, 0, 1), (chip, cross, 3, 2)):
            values = []
            for k in range(16):
                received = jnp.where(odd, upper[f, k], lower[f, k])
                value = part[f, plane, k] + 0.5 * (caz[beside, k] * received)
                values.append(edged(plane, k, value))
            for k in range(16):
                work[f, plane, k] = values[k]
        for a in (1, 2):
            values = [edged(a, k, part[f, a, k]) for k in range(16)]
            for k in range(16):
                work[f, a, k] = values[k]
        pltpu.make_async_copy(work.at[f], out.at[f], sems.at[f]).start()
        return carry

    lax.fori_loop(0, fields, field, 0)

    def drain(f, carry):
        pltpu.make_async_copy(work.at[f], out.at[f], sems.at[f]).wait()
        return carry

    lax.fori_loop(0, fields, drain, 0)


def finish(low, high, cross, chip, caz, part):
    fields = part.shape[0]
    return pl.pallas_call(
        finish_kernel,
        out_shape=arr(*part.shape),
        in_specs=[vmem] * 6,
        out_specs=in_hbm,
        scratch_shapes=[
            pltpu.VMEM(part.shape, jnp.float32),
            pltpu.SemaphoreType.DMA((fields,)),
        ],
        compiler_params=params(),
    )(low, high, cross, chip, caz, part)


def exchange(low, high, axis):
    count = lax.axis_size(axis)
    up = [(i, (i + 1) % count) for i in range(count)]
    down = [(j, i) for i, j in up]
    return lax.ppermute(high, axis, up), lax.ppermute(low, axis, down)


def pair(array, axis, crossing):
    count = lax.axis_size(axis)
    step = 1 if crossing else -1
    route = [(i, (i + step) % count if i % 2 else (i - step) % count) for i in range(count)]
    return lax.ppermute(array, axis, route)


def per_device(flow_state, velocity, inlet_state, radial_inflow, face_tags, decay_rates):
    fields = flow_state.shape[0]
    u = flow_state.reshape((fields, 4, 16) + tile)
    vel = velocity.reshape((3, 4, 16) + tile)
    inlet = inlet_state.reshape(fields, 16, 128)
    lane = lax.broadcasted_iota(jnp.int32, tile, 1)
    tags = jnp.where(lane == 0, face_tags[0].reshape(8, 1), face_tags[1].reshape(8, 1))
    inflow = radial_inflow.transpose(0, 2, 3, 4, 5, 1).reshape(2, 16, 8, fields)

    rows_low, rows_high, face_low, face_high = depart(u, vel)
    row_below, row_above = exchange(rows_low, rows_high, "axial")
    below, above = exchange(face_low, face_high, "azim")

    va, cax, crad, edge = prepare(tags, inflow, vel)
    acc = first_section(decay_rates, edge, u, va, cax, crad)
    factors, low, high = edges(1.0, inlet, rows_low, rows_high, row_below, row_above)
    s1, cross, chip, rows_low, rows_high, caz = close_first(
        low, high, below, above, u, va, acc
    )
    row_below, row_above = exchange(rows_low, rows_high, "axial")
    cross, chip = pair(cross, "azim", True), pair(chip, "azim", False)

    part = second_section(decay_rates, edge, u, s1, va, cax, crad, caz)
    _, low, high = edges(0.5, inlet, rows_low, rows_high, row_below, row_above, factors)
    out = finish(low, high, cross, chip, caz, part)
    return out.reshape(flow_state.shape)


def solution(mesh):
    in_specs = (
        P(None, None, None, None, "azim", "axial", None),
        P(None, None, None, None, "azim", "axial", None),
        P(None, None, None, "azim", None),
        P(None, None, None, None, "azim", "axial"),
        P(None, "azim", "axial"),
        P(),
    )
    out_specs = P(None, None, None, None, "azim", "axial", None)
    return jax.shard_map(
        per_device, mesh=mesh, in_specs=in_specs, out_specs=out_specs, check_vma=False
    )
```

time: 48.5 us -> 44.6 us (0.920)
  starting transfers between devices: 15.3 us -> 12.8 us
  Pallas kernels: 13.2 us -> 11.6 us
  waiting for transfers between devices: 14.6 us -> 15.9 us
  local copies, waits for them, and re-layouts: 4.47 us -> 3.91 us
    ppermute x8, starting transfers between devices: 15.3 us -> 12.8 us  [the longest x6 11.5 us: exchange(): return (lax.ppermute(high, axis, up), lax.ppermute(low, axis, down))]
    pallas_call x3, Pallas kernels: 2.03 us -> 0.33 us  [the longest x1 0.25 us: depart(): pl.pallas_call(depart_kernel, out_shape=[arr(fields + 1, 16, 128)] * 2 +...]
    pallas_call x1, Pallas kernels: 0.38 us -> 2.01 us  [prepare(): pl.pallas_call(prepare_kernel, out_shape=[arr(3, 4, 16, 8, 128), arr(4, 4...]
    ppermute x8, waiting for transfers between devices: 14.6 us -> 15.9 us  [the longest x6 15.7 us: exchange(): return (lax.ppermute(high, axis, up), lax.ppermute(low, axis, down))]
    pallas_call x1, Pallas kernels: 2.07 us -> 0.88 us  [close_first(): pl.pallas_call(close_kernel, out_shape=[arr(fields, 4, 16, 8, 128), arr(f...]
    unnamed x18 -> x16, local copies, waits for them, and re-layouts: 4.11 us -> 3.9 us
  transfers between devices with their start and end apart: 8 -> 8, of which waited for: 5 -> 5; matrix products, arithmetic and copies ran while one was open for 2% -> 0% of each run, Pallas kernels for 16% -> 20%
where the time goes in v2:
time: 44.6 us; the launch traced here: 44.4 us
  waiting for transfers between devices  15.9 us (36%)
  starting transfers between devices  12.8 us (29%)
  Pallas kernels  11.6 us (26%)
  local copies, waits for them, and re-layouts  3.91 us (9%)
    ppermute x6, waiting for transfers between devices, exchange(): return (lax.ppermute(high, axis, up), lax.ppermute(low, axis, down))  15.7 us
    ppermute x6, starting transfers between devices, exchange(): return (lax.ppermute(high, axis, up), lax.ppermute(low, axis, down))  11.5 us
    unnamed x16, local copies, waits for them, and re-layouts  3.9 us
    pallas_call x1, Pallas kernels, second_section(): pl.pallas_call(second_kernel, out_shape=arr(fields, 4, 16, 8, 128), in_sp...  3.5 us
    pallas_call x1, Pallas kernels, first_section(): pl.pallas_call(first_kernel, out_shape=arr(fields, 4, 16, 8, 128), in_spe...  3.18 us
    pallas_call x1, Pallas kernels, prepare(): pl.pallas_call(prepare_kernel, out_shape=[arr(3, 4, 16, 8, 128), arr(4, 4...  2.01 us
    pallas_call x1, Pallas kernels, finish(): pl.pallas_call(finish_kernel, out_shape=arr(*part.shape), in_specs=[vmem]...  1.71 us
    ppermute x2, starting transfers between devices, pair(): return lax.ppermute(array, axis, route)  1.31 us
  transfers between devices with their start and end apart: 8, of which 5 were waited for; matrix products, arithmetic and copies ran while one was open for 0% of the time, Pallas kernels for 20%

profile of v2, /device:TPU:0, one launch (start us, length us, event | category | flops | bytes accessed | tf_op | source)
XLA Modules:
  0.0 44.4 jit_solution(17128000125866821865)
XLA Ops:
  0.0 0.0 copy-start.7
  0.0 0.0 copy-start.6
  0.0 0.0 copy-start
  0.0 1.8 %copy-done = f32[11,4,4,4,1,8,128]{6,5,4,3,2,1,0:T(8,128)S(1)} copy-done((f32[11,4,4,4,1,8,128]{6,5,4,3,2,1,0:T(8,128)S(1)}, f32[11,4,4,4,1,8,128]{6,5,4,3,2,1,0:T(8,128)}, u32[]{:S(2)}) %copy-start) | copy-done | bytes 2883608
  1.8 0.0 copy-start.2
  1.8 1.1 %copy-done.2 = f32[3,4,4,4,1,8,128]{6,5,4,3,2,1,0:T(8,128)S(1)} copy-done((f32[3,4,4,4,1,8,128]{6,5,4,3,2,1,0:T(8,128)S(1)}, f32[3,4,4,4,1,8,128]{6,5,4,3,2,1,0:T(8,128)}, u32[]{:S(2)}) %copy-start.2) | copy-done | bytes 786456
  3.0 0.0 copy-start.3
  3.0 0.0 copy-start.1
  3.0 0.3 shard_map.64
  3.2 0.1 collective-permute-start.2
  3.3 6.1 %collective-permute-start.3 = (f32[12,16,8,128]{3,2,1,0:T(8,128)S(1)}, f32[12,16,8,128]{3,2,1,0:T(8,128)S(1)}, u32[]{:S(2)}, u32[]{:S(2)}) collective-permute-start(f32[12,16,8,128]{3,2,1,0:T(8,128)S(1)} %get-tuple-element.29), channel_id=1, source_target_pairs={{8,0},{16,8},{24,16},{32,24},{40,32},{48,40},{56,48},{64,56},{72,6... | collective-permute-start | bytes 2359304 | tf_op jit(solution)/shard_map/ppermute | solution.py:420
  9.4 3.3 %collective-permute-start.1 = (f32[12,16,128]{2,1,0:T(8,128)S(1)}, f32[12,16,128]{2,1,0:T(8,128)S(1)}, u32[]{:S(2)}, u32[]{:S(2)}) collective-permute-start(f32[12,16,128]{2,1,0:T(8,128)S(1)} %get-tuple-element.24.own_low), channel_id=1, source_target_pairs={{1,0},{2,1},{3,2},{4,3},{5,4},{6,5},{7,6},{0,7},{9,8},{10,9},{11,1... | collective-permute-start | bytes 294920 | tf_op jit(solution)/shard_map/ppermute | solution.py:420
  12.7 0.0 collective-permute-start
  12.7 0.0 copy-done.7
  12.7 0.1 broadcast_select_fusion.tags
  12.8 0.0 copy-done.3
  12.8 0.0 copy-start.5
  12.8 0.9 %copy-done.5 = f32[2,11,4,4,1,8]{1,5,4,3,2,0:T(8,128)S(1)} copy-done((f32[2,11,4,4,1,8]{1,5,4,3,2,0:T(8,128)S(1)}, f32[2,11,4,4,1,8]{1,5,4,3,2,0:T(8,128)}, u32[]{:S(2)}) %copy-start.5) | copy-done | bytes 11288
  13.7 2.0 %shard_map.66 = (f32[3,4,16,8,128]{4,3,2,1,0:T(8,128)S(1)}, f32[4,4,4,8,128]{4,3,2,1,0:T(8,128)S(1)}, f32[4,4,4,8,128]{4,3,2,1,0:T(8,128)S(1)}, f32[11,16,8,128]{3,2,1,0:T(8,128)S(1)}) custom-call(s32[8,128]{1,0:T(8,128)S(1)} %broadcast_select_fusion.tags, f32[2,16,8,11]{3,2,1,0:T(8,128)S(1)} %bitcast.21, f32[3,4,16,8,128]{4,3,2,1,0:T(8,128)S(1)} %bitcast.18), custom_call_target="tpu_custom_call" | custom-call | tf_op jit(solution)/shard_map/pallas_call | solution.py:138
  15.7 0.0 copy-done.6
  15.7 0.0 copy-done.1
  15.7 0.0 copy-start.4
  15.8 3.2 %shard_map.67.acc = f32[11,4,16,8,128]{4,3,2,1,0:T(8,128)S(1)} custom-call(f32[11]{0:T(128)S(1)} %copy-done.6, f32[11,16,8,128]{3,2,1,0:T(8,128)S(1)} %get-tuple-element.31.edge, f32[11,4,16,8,128]{4,3,2,1,0:T(8,128)S(1)} %bitcast.14, f32[3,4,16,8,128]{4,3,2,1,0:T(8,128)S(1)} %get-tuple-element.30.va, f32[4,4,4,8,128]{4,3,2,1,0:T(8,128)S(1)} %get-tuple-element.32.cax, ...), custom_call_target="tpu_custom_call" | custom-call | tf_op jit(solution)/shard_map/pallas_call | solution.py:200
  18.9 2.3 %collective-permute-done.1.above = f32[12,16,128]{2,1,0:T(8,128)S(1)} collective-permute-done((f32[12,16,128]{2,1,0:T(8,128)S(1)}, f32[12,16,128]{2,1,0:T(8,128)S(1)}, u32[]{:S(2)}, u32[]{:S(2)}) %collective-permute-start.1) | collective-permute-done | bytes 98336 | tf_op jit(solution)/shard_map/ppermute | solution.py:420
  21.3 4.1 %collective-permute-done.below = f32[12,16,128]{2,1,0:T(8,128)S(1)} collective-permute-done((f32[12,16,128]{2,1,0:T(8,128)S(1)}, f32[12,16,128]{2,1,0:T(8,128)S(1)}, u32[]{:S(2)}, u32[]{:S(2)}) %collective-permute-start) | collective-permute-done | bytes 98336 | tf_op jit(solution)/shard_map/ppermute | solution.py:420
  25.4 0.0 copy-done.4
  25.4 0.0 collective-permute-done.2.below
  25.4 0.0 collective-permute-done.3.above
  25.5 0.9 %shard_map.68 = (f32[11,4,16,8,128]{4,3,2,1,0:T(8,128)S(1)}, f32[11,16,8,128]{3,2,1,0:T(8,128)S(1)}, f32[11,16,8,128]{3,2,1,0:T(8,128)S(1)}, f32[11,16,128]{2,1,...) custom-call(f32[11,16,128]{2,1,0:T(8,128)S(1)} %get-tuple-element.26.lo, ...), custom_call_target="tpu_custom_call", output_to_operand_aliasing={{0}: (6, {})} | custom-call | tf_op jit(solution)/shard_map/pallas_call | solution.py:343
  26.3 1.3 %collective-permute-start.6 = (f32[11,16,8,128]{3,2,1,0:T(8,128)S(1)}, f32[11,16,8,128]{3,2,1,0:T(8,128)S(1)}, u32[]{:S(2)}, u32[]{:S(2)}) collective-permute-start(f32[11,16,8,128]{3,2,1,0:T(8,128)S(1)} %get-tuple-element.39), channel_id=1, source_target_pairs={{0,120},{8,16},{16,8},{24,32},{32,24},{40,48},{48,40},{56,64},{64,... | collective-permute-start | bytes 2162696 | tf_op jit(solution)/shard_map/ppermute | solution.py:427
  27.6 0.0 collective-permute-start.7
  27.7 1.7 %collective-permute-start.5 = (f32[11,16,128]{2,1,0:T(8,128)S(1)}, f32[11,16,128]{2,1,0:T(8,128)S(1)}, u32[]{:S(2)}, u32[]{:S(2)}) collective-permute-start(f32[11,16,128]{2,1,0:T(8,128)S(1)} %get-tuple-element.34.own_low), channel_id=1, source_target_pairs={{1,0},{2,1},{3,2},{4,3},{5,4},{6,5},{7,6},{0,7},{9,8},{10,9},{11,1... | collective-permute-start | bytes 270344 | tf_op jit(solution)/shard_map/ppermute | solution.py:420
  29.3 0.4 collective-permute-start.4
  29.7 3.5 %shard_map.70.part = f32[11,4,16,8,128]{4,3,2,1,0:T(8,128)S(1)} custom-call(f32[11]{0:T(128)S(1)} %copy-done.6, f32[11,16,8,128]{3,2,1,0:T(8,128)S(1)} %get-tuple-element.31.edge, f32[11,4,16,8,128]{4,3,2,1,0:T(8,128)S(1)} %bitcast.16, f32[11,4,16,8,128]{4,3,2,1,0:T(8,128)S(1)} %get-tuple-element.42.s1, f32[3,4,16,8,128]{4,3,2,1,0:T(8,128)S(1)} %get-tuple-element.30.va, ...), custom_call_target="tpu_custom_call" | custom-call | tf_op jit(solution)/shard_map/pallas_call | solution.py:236
  33.2 6.2 %collective-permute-done.5.above = f32[11,16,128]{2,1,0:T(8,128)S(1)} collective-permute-done((f32[11,16,128]{2,1,0:T(8,128)S(1)}, f32[11,16,128]{2,1,0:T(8,128)S(1)}, u32[]{:S(2)}, u32[]{:S(2)}) %collective-permute-start.5) | collective-permute-done | bytes 90144 | tf_op jit(solution)/shard_map/ppermute | solution.py:420
  39.4 3.1 %collective-permute-done.4.below = f32[11,16,128]{2,1,0:T(8,128)S(1)} collective-permute-done((f32[11,16,128]{2,1,0:T(8,128)S(1)}, f32[11,16,128]{2,1,0:T(8,128)S(1)}, u32[]{:S(2)}, u32[]{:S(2)}) %collective-permute-start.4) | collective-permute-done | bytes 90144 | tf_op jit(solution)/shard_map/ppermute | solution.py:420
  42.5 0.2 collective-permute-done.6.cross
  42.7 0.0 collective-permute-done.7.chip
  42.7 1.7 %shard_map.71 = f32[11,4,16,8,128]{4,3,2,1,0:T(8,128)} custom-call(f32[11,16,128]{2,1,0:T(8,128)S(1)} %get-tuple-element.37.low, f32[11,16,128]{2,1,0:T(8,128)S(1)} %get-tuple-element.38.high, f32[11,16,8,128]{3,2,1,0:T(8,128)S(1)} %collective-permute-done.6.cross, f32[11,16,8,128]{3,2,1,0:T(8,128)S(1)} %collective-permute-done.7.chip, ...), custom_call_target="tpu_custom_call" | custom-call | tf_op jit(solution)/shard_map/pallas_call | solution.py:403
  (4 shorter events, 0.1 us)
Async XLA Ops:
  0.0 12.7 %copy-start.7 = (s32[2,1,8]{2,1,0:T(1,128)S(1)}, s32[2,1,8]{2,1,0:T(1,128)}, u32[]{:S(2)}) copy-start(s32[2,1,8]{2,1,0:T(1,128)} %param.10) | copy-start | bytes 196
  0.0 15.7 %copy-start.6 = (f32[11]{0:T(128)S(1)}, f32[11]{0:T(128)}, u32[]{:S(2)}) copy-start(f32[11]{0:T(128)} %decay.3) | copy-start | bytes 136
  0.0 1.8 %copy-start = (f32[11,4,4,4,1,8,128]{6,5,4,3,2,1,0:T(8,128)S(1)}, f32[11,4,4,4,1,8,128]{6,5,4,3,2,1,0:T(8,128)}, u32[]{:S(2)}) copy-start(f32[11,4,4,4,1,8,128]{6,5,4,3,2,1,0:T(8,128)} %param.6) | copy-start | bytes 8650756
  1.8 1.1 %copy-start.2 = (f32[3,4,4,4,1,8,128]{6,5,4,3,2,1,0:T(8,128)S(1)}, f32[3,4,4,4,1,8,128]{6,5,4,3,2,1,0:T(8,128)}, u32[]{:S(2)}) copy-start(f32[3,4,4,4,1,8,128]{6,5,4,3,2,1,0:T(8,128)} %param.7) | copy-start | bytes 2359300
  3.0 9.8 %copy-start.3 = (f32[3,4,4,4,1,8,128]{6,5,4,3,2,1,0:T(8,128)S(1)}, f32[3,4,4,4,1,8,128]{6,5,4,3,2,1,0:T(8,128)}, u32[]{:S(2)}) copy-start(f32[3,4,4,4,1,8,128]{6,5,4,3,2,1,0:T(8,128)} %param.7) | copy-start | bytes 2359300
  3.0 12.8 %copy-start.1 = (f32[11,4,4,4,1,8,128]{6,5,4,3,2,1,0:T(8,128)S(1)}, f32[11,4,4,4,1,8,128]{6,5,4,3,2,1,0:T(8,128)}, u32[]{:S(2)}) copy-start(f32[11,4,4,4,1,8,128]{6,5,4,3,2,1,0:T(8,128)} %param.6) | copy-start | bytes 8650756
  3.2 22.2 %collective-permute-start.2 = (f32[12,16,8,128]{3,2,1,0:T(8,128)S(1)}, f32[12,16,8,128]{3,2,1,0:T(8,128)S(1)}, u32[]{:S(2)}, u32[]{:S(2)}) collective-permute-start(f32[12,16,8,128]{3,2,1,0:T(8,128)S(1)} %get-tuple-element.28), channel_id=1, source_target_pairs={{0,8},{8,16},{16,24},{24,32},{32,40},{40,48},{48,56},{56,64},{64,7... | collective-permute-start | bytes 2359304 | tf_op jit(solution)/shard_map/ppermute | solution.py:420
  3.3 22.1 %collective-permute-start.3 = (f32[12,16,8,128]{3,2,1,0:T(8,128)S(1)}, f32[12,16,8,128]{3,2,1,0:T(8,128)S(1)}, u32[]{:S(2)}, u32[]{:S(2)}) collective-permute-start(f32[12,16,8,128]{3,2,1,0:T(8,128)S(1)} %get-tuple-element.29), channel_id=1, source_target_pairs={{8,0},{16,8},{24,16},{32,24},{40,32},{48,40},{56,48},{64,56},{72,6... | collective-permute-start | bytes 2359304 | tf_op jit(solution)/shard_map/ppermute | solution.py:420
  9.4 11.8 %collective-permute-start.1 = (f32[12,16,128]{2,1,0:T(8,128)S(1)}, f32[12,16,128]{2,1,0:T(8,128)S(1)}, u32[]{:S(2)}, u32[]{:S(2)}) collective-permute-start(f32[12,16,128]{2,1,0:T(8,128)S(1)} %get-tuple-element.24.own_low), channel_id=1, source_target_pairs={{1,0},{2,1},{3,2},{4,3},{5,4},{6,5},{7,6},{0,7},{9,8},{10,9},{11,1... | collective-permute-start | bytes 294920 | tf_op jit(solution)/shard_map/ppermute | solution.py:420
  12.7 12.7 %collective-permute-start = (f32[12,16,128]{2,1,0:T(8,128)S(1)}, f32[12,16,128]{2,1,0:T(8,128)S(1)}, u32[]{:S(2)}, u32[]{:S(2)}) collective-permute-start(f32[12,16,128]{2,1,0:T(8,128)S(1)} %get-tuple-element.25.own_high), channel_id=1, source_target_pairs={{0,1},{1,2},{2,3},{3,4},{4,5},{5,6},{6,7},{7,0},{8,9},{9,10},{10,1... | collective-permute-start | bytes 294920 | tf_op jit(solution)/shard_map/ppermute | solution.py:420
  12.8 0.9 %copy-start.5 = (f32[2,11,4,4,1,8]{1,5,4,3,2,0:T(8,128)S(1)}, f32[2,11,4,4,1,8]{1,5,4,3,2,0:T(8,128)}, u32[]{:S(2)}) copy-start(f32[2,11,4,4,1,8]{1,5,4,3,2,0:T(8,128)} %param.9) | copy-start | bytes 33796
  15.7 9.6 %copy-start.4 = (f32[11,4,4,1,128]{4,3,2,1,0:T(1,128)S(1)}, f32[11,4,4,1,128]{4,3,2,1,0:T(1,128)}, u32[]{:S(2)}) copy-start(f32[11,4,4,1,128]{4,3,2,1,0:T(1,128)} %param.8) | copy-start | bytes 270340
  26.3 16.3 %collective-permute-start.6 = (f32[11,16,8,128]{3,2,1,0:T(8,128)S(1)}, f32[11,16,8,128]{3,2,1,0:T(8,128)S(1)}, u32[]{:S(2)}, u32[]{:S(2)}) collective-permute-start(f32[11,16,8,128]{3,2,1,0:T(8,128)S(1)} %get-tuple-element.39), channel_id=1, source_target_pairs={{0,120},{8,16},{16,8},{24,32},{32,24},{40,48},{48,40},{56,64},{64,... | collective-permute-start | bytes 2162696 | tf_op jit(solution)/shard_map/ppermute | solution.py:427
  27.6 15.0 %collective-permute-start.7 = (f32[11,16,8,128]{3,2,1,0:T(8,128)S(1)}, f32[11,16,8,128]{3,2,1,0:T(8,128)S(1)}, u32[]{:S(2)}, u32[]{:S(2)}) collective-permute-start(f32[11,16,8,128]{3,2,1,0:T(8,128)S(1)} %get-tuple-element.40), channel_id=1, source_target_pairs={{0,8},{8,0},{16,24},{24,16},{32,40},{40,32},{48,56},{56,48},{64,72... | collective-permute-start | bytes 2162696 | tf_op jit(solution)/shard_map/ppermute | solution.py:427
  27.7 11.7 %collective-permute-start.5 = (f32[11,16,128]{2,1,0:T(8,128)S(1)}, f32[11,16,128]{2,1,0:T(8,128)S(1)}, u32[]{:S(2)}, u32[]{:S(2)}) collective-permute-start(f32[11,16,128]{2,1,0:T(8,128)S(1)} %get-tuple-element.34.own_low), channel_id=1, source_target_pairs={{1,0},{2,1},{3,2},{4,3},{5,4},{6,5},{7,6},{0,7},{9,8},{10,9},{11,1... | collective-permute-start | bytes 270344 | tf_op jit(solution)/shard_map/ppermute | solution.py:420
  29.3 13.1 %collective-permute-start.4 = (f32[11,16,128]{2,1,0:T(8,128)S(1)}, f32[11,16,128]{2,1,0:T(8,128)S(1)}, u32[]{:S(2)}, u32[]{:S(2)}) collective-permute-start(f32[11,16,128]{2,1,0:T(8,128)S(1)} %get-tuple-element.35.own_high), channel_id=1, source_target_pairs={{0,1},{1,2},{2,3},{3,4},{4,5},{5,6},{6,7},{7,0},{8,9},{9,10},{10,1... | collective-permute-start | bytes 270344 | tf_op jit(solution)/shard_map/ppermute | solution.py:420

commit v3 on v2

--- a/solution.py
+++ b/solution.py
@@ -358,7 +358,7 @@
 
 
 def finish_kernel(
-    low, high, cross, chip, caz, part, out, work, sems
+    low, high, chip, cross, caz, part, out, work, sems
 ):
     fields = part.shape[0]
     sub = lax.broadcasted_iota(jnp.int32, tile, 0)
@@ -398,7 +398,7 @@
     lax.fori_loop(0, fields, drain, 0)
 
 
-def finish(low, high, cross, chip, caz, part):
+def finish(low, high, chip, cross, caz, part):
     fields = part.shape[0]
     return pl.pallas_call(
         finish_kernel,
@@ -410,7 +410,7 @@
             pltpu.SemaphoreType.DMA((fields,)),
         ],
         compiler_params=params(),
-    )(low, high, cross, chip, caz, part)
+    )(low, high, chip, cross, caz, part)
 
 
 def exchange(low, high, axis):
@@ -447,11 +447,11 @@
         low, high, below, above, u, va, acc
     )
     row_below, row_above = exchange(rows_low, rows_high, "axial")
-    cross, chip = pair(cross, "azim", True), pair(chip, "azim", False)
+    chip, cross = pair(chip, "azim", False), pair(cross, "azim", True)
 
     part = second_section(decay_rates, edge, u, s1, va, cax, crad, caz)
     _, low, high = edges(0.5, inlet, rows_low, rows_high, row_below, row_above, factors)
-    out = finish(low, high, cross, chip, caz, part)
+    out = finish(low, high, chip, cross, caz, part)
     return out.reshape(flow_state.shape)
 
 

time: 44.6 us -> 43.5 us (0.975)
  waiting for transfers between devices: 15.9 us -> 14.7 us
    ppermute x6, waiting for transfers between devices: 15.7 us -> 14.7 us  [exchange(): return (lax.ppermute(high, axis, up), lax.ppermute(low, axis, down))]
  transfers between devices with their start and end apart: 8 -> 8, of which waited for: 5 -> 4; matrix products, arithmetic and copies ran while one was open for 0% -> 0% of each run, Pallas kernels for 20% -> 20%
where the time goes in v3:
time: 43.5 us; the launch traced here: 43.3 us
  waiting for transfers between devices  14.7 us (34%)
  starting transfers between devices  12.9 us (30%)
  Pallas kernels  11.6 us (27%)
  local copies, waits for them, and re-layouts  3.91 us (9%)
    ppermute x6, waiting for transfers between devices, exchange(): return (lax.ppermute(high, axis, up), lax.ppermute(low, axis, down))  14.7 us
    ppermute x6, starting transfers between devices, exchange(): return (lax.ppermute(high, axis, up), lax.ppermute(low, axis, down))  11.5 us
    unnamed x16, local copies, waits for them, and re-layouts  3.9 us
    pallas_call x1, Pallas kernels, second_section(): pl.pallas_call(second_kernel, out_shape=arr(fields, 4, 16, 8, 128), in_sp...  3.5 us
    pallas_call x1, Pallas kernels, first_section(): pl.pallas_call(first_kernel, out_shape=arr(fields, 4, 16, 8, 128), in_spe...  3.18 us
    pallas_call x1, Pallas kernels, prepare(): pl.pallas_call(prepare_kernel, out_shape=[arr(3, 4, 16, 8, 128), arr(4, 4...  2.01 us
    pallas_call x1, Pallas kernels, finish(): pl.pallas_call(finish_kernel, out_shape=arr(*part.shape), in_specs=[vmem]...  1.72 us
    ppermute x2, starting transfers between devices, pair(): return lax.ppermute(array, axis, route)  1.39 us
  transfers between devices with their start and end apart: 8, of which 4 were waited for; matrix products, arithmetic and copies ran while one was open for 0% of the time, Pallas kernels for 20%

profile of v3, /device:TPU:0, one launch (start us, length us, event | category | flops | bytes accessed | tf_op | source)
XLA Modules:
  0.0 43.3 jit_solution(15883788308466979076)
XLA Ops:
  0.0 0.0 copy-start.7
  0.0 0.0 copy-start.6
  0.0 0.0 copy-start
  0.0 1.8 %copy-done = f32[11,4,4,4,1,8,128]{6,5,4,3,2,1,0:T(8,128)S(1)} copy-done((f32[11,4,4,4,1,8,128]{6,5,4,3,2,1,0:T(8,128)S(1)}, f32[11,4,4,4,1,8,128]{6,5,4,3,2,1,0:T(8,128)}, u32[]{:S(2)}) %copy-start) | copy-done | bytes 2883608
  1.8 0.0 copy-start.2
  1.8 1.1 %copy-done.2 = f32[3,4,4,4,1,8,128]{6,5,4,3,2,1,0:T(8,128)S(1)} copy-done((f32[3,4,4,4,1,8,128]{6,5,4,3,2,1,0:T(8,128)S(1)}, f32[3,4,4,4,1,8,128]{6,5,4,3,2,1,0:T(8,128)}, u32[]{:S(2)}) %copy-start.2) | copy-done | bytes 786456
  3.0 0.0 copy-start.3
  3.0 0.0 copy-start.1
  3.0 0.3 shard_map.64
  3.2 0.1 collective-permute-start.2
  3.3 6.1 %collective-permute-start.3 = (f32[12,16,8,128]{3,2,1,0:T(8,128)S(1)}, f32[12,16,8,128]{3,2,1,0:T(8,128)S(1)}, u32[]{:S(2)}, u32[]{:S(2)}) collective-permute-start(f32[12,16,8,128]{3,2,1,0:T(8,128)S(1)} %get-tuple-element.29), channel_id=1, source_target_pairs={{8,0},{16,8},{24,16},{32,24},{40,32},{48,40},{56,48},{64,56},{72,6... | collective-permute-start | bytes 2359304 | tf_op jit(solution)/shard_map/ppermute | solution.py:420
  9.4 3.3 %collective-permute-start.1 = (f32[12,16,128]{2,1,0:T(8,128)S(1)}, f32[12,16,128]{2,1,0:T(8,128)S(1)}, u32[]{:S(2)}, u32[]{:S(2)}) collective-permute-start(f32[12,16,128]{2,1,0:T(8,128)S(1)} %get-tuple-element.24.own_low), channel_id=1, source_target_pairs={{1,0},{2,1},{3,2},{4,3},{5,4},{6,5},{7,6},{0,7},{9,8},{10,9},{11,1... | collective-permute-start | bytes 294920 | tf_op jit(solution)/shard_map/ppermute | solution.py:420
  12.7 0.0 collective-permute-start
  12.7 0.0 copy-done.7
  12.7 0.1 broadcast_select_fusion.tags
  12.8 0.0 copy-done.3
  12.8 0.0 copy-start.5
  12.8 0.9 %copy-done.5 = f32[2,11,4,4,1,8]{1,5,4,3,2,0:T(8,128)S(1)} copy-done((f32[2,11,4,4,1,8]{1,5,4,3,2,0:T(8,128)S(1)}, f32[2,11,4,4,1,8]{1,5,4,3,2,0:T(8,128)}, u32[]{:S(2)}) %copy-start.5) | copy-done | bytes 11288
  13.7 2.0 %shard_map.66 = (f32[3,4,16,8,128]{4,3,2,1,0:T(8,128)S(1)}, f32[4,4,4,8,128]{4,3,2,1,0:T(8,128)S(1)}, f32[4,4,4,8,128]{4,3,2,1,0:T(8,128)S(1)}, f32[11,16,8,128]{3,2,1,0:T(8,128)S(1)}) custom-call(s32[8,128]{1,0:T(8,128)S(1)} %broadcast_select_fusion.tags, f32[2,16,8,11]{3,2,1,0:T(8,128)S(1)} %bitcast.21, f32[3,4,16,8,128]{4,3,2,1,0:T(8,128)S(1)} %bitcast.18), custom_call_target="tpu_custom_call" | custom-call | tf_op jit(solution)/shard_map/pallas_call | solution.py:138
  15.7 0.0 copy-done.6
  15.7 0.0 copy-done.1
  15.7 0.0 copy-start.4
  15.8 3.2 %shard_map.67.acc = f32[11,4,16,8,128]{4,3,2,1,0:T(8,128)S(1)} custom-call(f32[11]{0:T(128)S(1)} %copy-done.6, f32[11,16,8,128]{3,2,1,0:T(8,128)S(1)} %get-tuple-element.31.edge, f32[11,4,16,8,128]{4,3,2,1,0:T(8,128)S(1)} %bitcast.14, f32[3,4,16,8,128]{4,3,2,1,0:T(8,128)S(1)} %get-tuple-element.30.va, f32[4,4,4,8,128]{4,3,2,1,0:T(8,128)S(1)} %get-tuple-element.32.cax, ...), custom_call_target="tpu_custom_call" | custom-call | tf_op jit(solution)/shard_map/pallas_call | solution.py:200
  18.9 2.3 %collective-permute-done.1.above = f32[12,16,128]{2,1,0:T(8,128)S(1)} collective-permute-done((f32[12,16,128]{2,1,0:T(8,128)S(1)}, f32[12,16,128]{2,1,0:T(8,128)S(1)}, u32[]{:S(2)}, u32[]{:S(2)}) %collective-permute-start.1) | collective-permute-done | bytes 98336 | tf_op jit(solution)/shard_map/ppermute | solution.py:420
  21.3 4.1 %collective-permute-done.below = f32[12,16,128]{2,1,0:T(8,128)S(1)} collective-permute-done((f32[12,16,128]{2,1,0:T(8,128)S(1)}, f32[12,16,128]{2,1,0:T(8,128)S(1)}, u32[]{:S(2)}, u32[]{:S(2)}) %collective-permute-start) | collective-permute-done | bytes 98336 | tf_op jit(solution)/shard_map/ppermute | solution.py:420
  25.4 0.0 copy-done.4
  25.4 0.0 collective-permute-done.2.below
  25.4 0.0 collective-permute-done.3.above
  25.5 0.9 %shard_map.68 = (f32[11,4,16,8,128]{4,3,2,1,0:T(8,128)S(1)}, f32[11,16,8,128]{3,2,1,0:T(8,128)S(1)}, f32[11,16,8,128]{3,2,1,0:T(8,128)S(1)}, f32[11,16,128]{2,1,...) custom-call(f32[11,16,128]{2,1,0:T(8,128)S(1)} %get-tuple-element.26.lo, ...), custom_call_target="tpu_custom_call", output_to_operand_aliasing={{0}: (6, {})} | custom-call | tf_op jit(solution)/shard_map/pallas_call | solution.py:343
  26.3 0.1 collective-permute-start.6
  26.4 1.3 %collective-permute-start.7 = (f32[11,16,8,128]{3,2,1,0:T(8,128)S(1)}, f32[11,16,8,128]{3,2,1,0:T(8,128)S(1)}, u32[]{:S(2)}, u32[]{:S(2)}) collective-permute-start(f32[11,16,8,128]{3,2,1,0:T(8,128)S(1)} %get-tuple-element.40), channel_id=1, source_target_pairs={{0,120},{8,16},{16,8},{24,32},{32,24},{40,48},{48,40},{56,64},{64,... | collective-permute-start | bytes 2162696 | tf_op jit(solution)/shard_map/ppermute | solution.py:427
  27.7 1.7 %collective-permute-start.5 = (f32[11,16,128]{2,1,0:T(8,128)S(1)}, f32[11,16,128]{2,1,0:T(8,128)S(1)}, u32[]{:S(2)}, u32[]{:S(2)}) collective-permute-start(f32[11,16,128]{2,1,0:T(8,128)S(1)} %get-tuple-element.34.own_low), channel_id=1, source_target_pairs={{1,0},{2,1},{3,2},{4,3},{5,4},{6,5},{7,6},{0,7},{9,8},{10,9},{11,1... | collective-permute-start | bytes 270344 | tf_op jit(solution)/shard_map/ppermute | solution.py:420
  29.4 0.4 collective-permute-start.4
  29.8 3.5 %shard_map.70.part = f32[11,4,16,8,128]{4,3,2,1,0:T(8,128)S(1)} custom-call(f32[11]{0:T(128)S(1)} %copy-done.6, f32[11,16,8,128]{3,2,1,0:T(8,128)S(1)} %get-tuple-element.31.edge, f32[11,4,16,8,128]{4,3,2,1,0:T(8,128)S(1)} %bitcast.16, f32[11,4,16,8,128]{4,3,2,1,0:T(8,128)S(1)} %get-tuple-element.42.s1, f32[3,4,16,8,128]{4,3,2,1,0:T(8,128)S(1)} %get-tuple-element.30.va, ...), custom_call_target="tpu_custom_call" | custom-call | tf_op jit(solution)/shard_map/pallas_call | solution.py:236
  33.3 5.2 %collective-permute-done.5.above = f32[11,16,128]{2,1,0:T(8,128)S(1)} collective-permute-done((f32[11,16,128]{2,1,0:T(8,128)S(1)}, f32[11,16,128]{2,1,0:T(8,128)S(1)}, u32[]{:S(2)}, u32[]{:S(2)}) %collective-permute-start.5) | collective-permute-done | bytes 90144 | tf_op jit(solution)/shard_map/ppermute | solution.py:420
  38.5 3.1 %collective-permute-done.4.below = f32[11,16,128]{2,1,0:T(8,128)S(1)} collective-permute-done((f32[11,16,128]{2,1,0:T(8,128)S(1)}, f32[11,16,128]{2,1,0:T(8,128)S(1)}, u32[]{:S(2)}, u32[]{:S(2)}) %collective-permute-start.4) | collective-permute-done | bytes 90144 | tf_op jit(solution)/shard_map/ppermute | solution.py:420
  41.6 0.0 collective-permute-done.6.chip
  41.6 0.0 collective-permute-done.7.cross
  41.6 1.7 %shard_map.71 = f32[11,4,16,8,128]{4,3,2,1,0:T(8,128)} custom-call(f32[11,16,128]{2,1,0:T(8,128)S(1)} %get-tuple-element.37.low, f32[11,16,128]{2,1,0:T(8,128)S(1)} %get-tuple-element.38.high, f32[11,16,8,128]{3,2,1,0:T(8,128)S(1)} %collective-permute-done.6.chip, f32[11,16,8,128]{3,2,1,0:T(8,128)S(1)} %collective-permute-done.7.cross, ...), custom_call_target="tpu_custom_call" | custom-call | tf_op jit(solution)/shard_map/pallas_call | solution.py:403
  (4 shorter events, 0.1 us)
Async XLA Ops:
  0.0 12.7 %copy-start.7 = (s32[2,1,8]{2,1,0:T(1,128)S(1)}, s32[2,1,8]{2,1,0:T(1,128)}, u32[]{:S(2)}) copy-start(s32[2,1,8]{2,1,0:T(1,128)} %param.10) | copy-start | bytes 196
  0.0 15.7 %copy-start.6 = (f32[11]{0:T(128)S(1)}, f32[11]{0:T(128)}, u32[]{:S(2)}) copy-start(f32[11]{0:T(128)} %decay.3) | copy-start | bytes 136
  0.0 1.8 %copy-start = (f32[11,4,4,4,1,8,128]{6,5,4,3,2,1,0:T(8,128)S(1)}, f32[11,4,4,4,1,8,128]{6,5,4,3,2,1,0:T(8,128)}, u32[]{:S(2)}) copy-start(f32[11,4,4,4,1,8,128]{6,5,4,3,2,1,0:T(8,128)} %param.6) | copy-start | bytes 8650756
  1.8 1.1 %copy-start.2 = (f32[3,4,4,4,1,8,128]{6,5,4,3,2,1,0:T(8,128)S(1)}, f32[3,4,4,4,1,8,128]{6,5,4,3,2,1,0:T(8,128)}, u32[]{:S(2)}) copy-start(f32[3,4,4,4,1,8,128]{6,5,4,3,2,1,0:T(8,128)} %param.7) | copy-start | bytes 2359300
  3.0 9.8 %copy-start.3 = (f32[3,4,4,4,1,8,128]{6,5,4,3,2,1,0:T(8,128)S(1)}, f32[3,4,4,4,1,8,128]{6,5,4,3,2,1,0:T(8,128)}, u32[]{:S(2)}) copy-start(f32[3,4,4,4,1,8,128]{6,5,4,3,2,1,0:T(8,128)} %param.7) | copy-start | bytes 2359300
  3.0 12.8 %copy-start.1 = (f32[11,4,4,4,1,8,128]{6,5,4,3,2,1,0:T(8,128)S(1)}, f32[11,4,4,4,1,8,128]{6,5,4,3,2,1,0:T(8,128)}, u32[]{:S(2)}) copy-start(f32[11,4,4,4,1,8,128]{6,5,4,3,2,1,0:T(8,128)} %param.6) | copy-start | bytes 8650756
  3.2 22.2 %collective-permute-start.2 = (f32[12,16,8,128]{3,2,1,0:T(8,128)S(1)}, f32[12,16,8,128]{3,2,1,0:T(8,128)S(1)}, u32[]{:S(2)}, u32[]{:S(2)}) collective-permute-start(f32[12,16,8,128]{3,2,1,0:T(8,128)S(1)} %get-tuple-element.28), channel_id=1, source_target_pairs={{0,8},{8,16},{16,24},{24,32},{32,40},{40,48},{48,56},{56,64},{64,7... | collective-permute-start | bytes 2359304 | tf_op jit(solution)/shard_map/ppermute | solution.py:420
  3.3 22.1 %collective-permute-start.3 = (f32[12,16,8,128]{3,2,1,0:T(8,128)S(1)}, f32[12,16,8,128]{3,2,1,0:T(8,128)S(1)}, u32[]{:S(2)}, u32[]{:S(2)}) collective-permute-start(f32[12,16,8,128]{3,2,1,0:T(8,128)S(1)} %get-tuple-element.29), channel_id=1, source_target_pairs={{8,0},{16,8},{24,16},{32,24},{40,32},{48,40},{56,48},{64,56},{72,6... | collective-permute-start | bytes 2359304 | tf_op jit(solution)/shard_map/ppermute | solution.py:420
  9.4 11.8 %collective-permute-start.1 = (f32[12,16,128]{2,1,0:T(8,128)S(1)}, f32[12,16,128]{2,1,0:T(8,128)S(1)}, u32[]{:S(2)}, u32[]{:S(2)}) collective-permute-start(f32[12,16,128]{2,1,0:T(8,128)S(1)} %get-tuple-element.24.own_low), channel_id=1, source_target_pairs={{1,0},{2,1},{3,2},{4,3},{5,4},{6,5},{7,6},{0,7},{9,8},{10,9},{11,1... | collective-permute-start | bytes 294920 | tf_op jit(solution)/shard_map/ppermute | solution.py:420
  12.7 12.7 %collective-permute-start = (f32[12,16,128]{2,1,0:T(8,128)S(1)}, f32[12,16,128]{2,1,0:T(8,128)S(1)}, u32[]{:S(2)}, u32[]{:S(2)}) collective-permute-start(f32[12,16,128]{2,1,0:T(8,128)S(1)} %get-tuple-element.25.own_high), channel_id=1, source_target_pairs={{0,1},{1,2},{2,3},{3,4},{4,5},{5,6},{6,7},{7,0},{8,9},{9,10},{10,1... | collective-permute-start | bytes 294920 | tf_op jit(solution)/shard_map/ppermute | solution.py:420
  12.8 0.9 %copy-start.5 = (f32[2,11,4,4,1,8]{1,5,4,3,2,0:T(8,128)S(1)}, f32[2,11,4,4,1,8]{1,5,4,3,2,0:T(8,128)}, u32[]{:S(2)}) copy-start(f32[2,11,4,4,1,8]{1,5,4,3,2,0:T(8,128)} %param.9) | copy-start | bytes 33796
  15.7 9.6 %copy-start.4 = (f32[11,4,4,1,128]{4,3,2,1,0:T(1,128)S(1)}, f32[11,4,4,1,128]{4,3,2,1,0:T(1,128)}, u32[]{:S(2)}) copy-start(f32[11,4,4,1,128]{4,3,2,1,0:T(1,128)} %param.8) | copy-start | bytes 270340
  26.3 15.3 %collective-permute-start.6 = (f32[11,16,8,128]{3,2,1,0:T(8,128)S(1)}, f32[11,16,8,128]{3,2,1,0:T(8,128)S(1)}, u32[]{:S(2)}, u32[]{:S(2)}) collective-permute-start(f32[11,16,8,128]{3,2,1,0:T(8,128)S(1)} %get-tuple-element.39), channel_id=1, source_target_pairs={{0,8},{8,0},{16,24},{24,16},{32,40},{40,32},{48,56},{56,48},{64,72... | collective-permute-start | bytes 2162696 | tf_op jit(solution)/shard_map/ppermute | solution.py:427
  26.4 15.2 %collective-permute-start.7 = (f32[11,16,8,128]{3,2,1,0:T(8,128)S(1)}, f32[11,16,8,128]{3,2,1,0:T(8,128)S(1)}, u32[]{:S(2)}, u32[]{:S(2)}) collective-permute-start(f32[11,16,8,128]{3,2,1,0:T(8,128)S(1)} %get-tuple-element.40), channel_id=1, source_target_pairs={{0,120},{8,16},{16,8},{24,32},{32,24},{40,48},{48,40},{56,64},{64,... | collective-permute-start | bytes 2162696 | tf_op jit(solution)/shard_map/ppermute | solution.py:427
  27.7 10.8 %collective-permute-start.5 = (f32[11,16,128]{2,1,0:T(8,128)S(1)}, f32[11,16,128]{2,1,0:T(8,128)S(1)}, u32[]{:S(2)}, u32[]{:S(2)}) collective-permute-start(f32[11,16,128]{2,1,0:T(8,128)S(1)} %get-tuple-element.34.own_low), channel_id=1, source_target_pairs={{1,0},{2,1},{3,2},{4,3},{5,4},{6,5},{7,6},{0,7},{9,8},{10,9},{11,1... | collective-permute-start | bytes 270344 | tf_op jit(solution)/shard_map/ppermute | solution.py:420
  29.4 12.2 %collective-permute-start.4 = (f32[11,16,128]{2,1,0:T(8,128)S(1)}, f32[11,16,128]{2,1,0:T(8,128)S(1)}, u32[]{:S(2)}, u32[]{:S(2)}) collective-permute-start(f32[11,16,128]{2,1,0:T(8,128)S(1)} %get-tuple-element.35.own_high), channel_id=1, source_target_pairs={{0,1},{1,2},{2,3},{3,4},{4,5},{5,6},{6,7},{7,0},{8,9},{9,10},{10,1... | collective-permute-start | bytes 270344 | tf_op jit(solution)/shard_map/ppermute | solution.py:420

commit v4 on v3

--- a/solution.py
+++ b/solution.py
@@ -364,6 +364,27 @@
     sub = lax.broadcasted_iota(jnp.int32, tile, 0)
     odd = azim_odd()
 
+    def copy(src, f, planes, nodes, sem):
+        at = (f, pl.ds(*planes), pl.ds(*nodes))
+        return pltpu.make_async_copy(src.at[at], out.at[at], sems.at[f, sem])
+
+    def early(f):
+        return copy(part, f, (1, 2), (4, 8), 0)
+
+    def late(f):
+        return [
+            copy(work, f, (0, 1), (0, 16), 1),
+            copy(work, f, (3, 1), (0, 16), 2),
+            copy(work, f, (1, 2), (0, 4), 3),
+            copy(work, f, (1, 2), (12, 4), 4),
+        ]
+
+    def begin(f, carry):
+        early(f).start()
+        return carry
+
+    lax.fori_loop(0, fields, begin, 0)
+
     def field(f, carry):
         def edged(a, k, value):
             if k < 4:
@@ -382,17 +403,21 @@
                 values.append(edged(plane, k, value))
             for k in range(16):
                 work[f, plane, k] = values[k]
+        outer = (0, 1, 2, 3, 12, 13, 14, 15)
         for a in (1, 2):
-            values = [edged(a, k, part[f, a, k]) for k in range(16)]
-            for k in range(16):
-                work[f, a, k] = values[k]
-        pltpu.make_async_copy(work.at[f], out.at[f], sems.at[f]).start()
+            values = [edged(a, k, part[f, a, k]) for k in outer]
+            for k, value in zip(outer, values):
+                work[f, a, k] = value
+        for c in late(f):
+            c.start()
         return carry
 
     lax.fori_loop(0, fields, field, 0)
 
     def drain(f, carry):
-        pltpu.make_async_copy(work.at[f], out.at[f], sems.at[f]).wait()
+        early(f).wait()
+        for c in late(f):
+            c.wait()
         return carry
 
     lax.fori_loop(0, fields, drain, 0)
@@ -407,7 +432,7 @@
         out_specs=in_hbm,
         scratch_shapes=[
             pltpu.VMEM(part.shape, jnp.float32),
-            pltpu.SemaphoreType.DMA((fields,)),
+            pltpu.SemaphoreType.DMA((fields, 5)),
         ],
         compiler_params=params(),
     )(low, high, chip, cross, caz, part)

time: 43.5 us -> 43.9 us (level)
  no operation moved by 1% of the time
where the time goes in v4:
time: 43.9 us; the launch traced here: 43.7 us
  waiting for transfers between devices  14.7 us (33%)
  starting transfers between devices  12.9 us (29%)
  Pallas kernels  11.9 us (27%)
  local copies, waits for them, and re-layouts  3.91 us (9%)
    ppermute x6, waiting for transfers between devices, exchange(): return (lax.ppermute(high, axis, up), lax.ppermute(low, axis, down))  14.7 us
    ppermute x6, starting transfers between devices, exchange(): return (lax.ppermute(high, axis, up), lax.ppermute(low, axis, down))  11.5 us
    unnamed x16, local copies, waits for them, and re-layouts  3.9 us
    pallas_call x1, Pallas kernels, second_section(): pl.pallas_call(second_kernel, out_shape=arr(fields, 4, 16, 8, 128), in_sp...  3.5 us
    pallas_call x1, Pallas kernels, first_section(): pl.pallas_call(first_kernel, out_shape=arr(fields, 4, 16, 8, 128), in_spe...  3.18 us
    pallas_call x1, Pallas kernels, finish(): pl.pallas_call(finish_kernel, out_shape=arr(*part.shape), in_specs=[vmem]...  2.04 us
    pallas_call x1, Pallas kernels, prepare(): pl.pallas_call(prepare_kernel, out_shape=[arr(3, 4, 16, 8, 128), arr(4, 4...  2.01 us
    ppermute x2, starting transfers between devices, pair(): return lax.ppermute(array, axis, route)  1.39 us
  transfers between devices with their start and end apart: 8, of which 4 were waited for; matrix products, arithmetic and copies ran while one was open for 0% of the time, Pallas kernels for 20%

profile of v4, /device:TPU:0, one launch (start us, length us, event | category | flops | bytes accessed | tf_op | source)
XLA Modules:
  0.0 43.7 jit_solution(12803433103182956998)
XLA Ops:
  0.0 0.0 copy-start.7
  0.0 0.0 copy-start.6
  0.0 0.0 copy-start
  0.0 1.8 %copy-done = f32[11,4,4,4,1,8,128]{6,5,4,3,2,1,0:T(8,128)S(1)} copy-done((f32[11,4,4,4,1,8,128]{6,5,4,3,2,1,0:T(8,128)S(1)}, f32[11,4,4,4,1,8,128]{6,5,4,3,2,1,0:T(8,128)}, u32[]{:S(2)}) %copy-start) | copy-done | bytes 2883608
  1.8 0.0 copy-start.2
  1.8 1.1 %copy-done.2 = f32[3,4,4,4,1,8,128]{6,5,4,3,2,1,0:T(8,128)S(1)} copy-done((f32[3,4,4,4,1,8,128]{6,5,4,3,2,1,0:T(8,128)S(1)}, f32[3,4,4,4,1,8,128]{6,5,4,3,2,1,0:T(8,128)}, u32[]{:S(2)}) %copy-start.2) | copy-done | bytes 786456
  3.0 0.0 copy-start.3
  3.0 0.0 copy-start.1
  3.0 0.3 shard_map.64
  3.2 0.1 collective-permute-start.2
  3.3 6.1 %collective-permute-start.3 = (f32[12,16,8,128]{3,2,1,0:T(8,128)S(1)}, f32[12,16,8,128]{3,2,1,0:T(8,128)S(1)}, u32[]{:S(2)}, u32[]{:S(2)}) collective-permute-start(f32[12,16,8,128]{3,2,1,0:T(8,128)S(1)} %get-tuple-element.29), channel_id=1, source_target_pairs={{8,0},{16,8},{24,16},{32,24},{40,32},{48,40},{56,48},{64,56},{72,6... | collective-permute-start | bytes 2359304 | tf_op jit(solution)/shard_map/ppermute | solution.py:445
  9.4 3.3 %collective-permute-start.1 = (f32[12,16,128]{2,1,0:T(8,128)S(1)}, f32[12,16,128]{2,1,0:T(8,128)S(1)}, u32[]{:S(2)}, u32[]{:S(2)}) collective-permute-start(f32[12,16,128]{2,1,0:T(8,128)S(1)} %get-tuple-element.24.own_low), channel_id=1, source_target_pairs={{1,0},{2,1},{3,2},{4,3},{5,4},{6,5},{7,6},{0,7},{9,8},{10,9},{11,1... | collective-permute-start | bytes 294920 | tf_op jit(solution)/shard_map/ppermute | solution.py:445
  12.7 0.0 collective-permute-start
  12.7 0.0 copy-done.7
  12.7 0.1 broadcast_select_fusion.tags
  12.8 0.0 copy-done.3
  12.8 0.0 copy-start.5
  12.8 0.9 %copy-done.5 = f32[2,11,4,4,1,8]{1,5,4,3,2,0:T(8,128)S(1)} copy-done((f32[2,11,4,4,1,8]{1,5,4,3,2,0:T(8,128)S(1)}, f32[2,11,4,4,1,8]{1,5,4,3,2,0:T(8,128)}, u32[]{:S(2)}) %copy-start.5) | copy-done | bytes 11288
  13.7 2.0 %shard_map.66 = (f32[3,4,16,8,128]{4,3,2,1,0:T(8,128)S(1)}, f32[4,4,4,8,128]{4,3,2,1,0:T(8,128)S(1)}, f32[4,4,4,8,128]{4,3,2,1,0:T(8,128)S(1)}, f32[11,16,8,128]{3,2,1,0:T(8,128)S(1)}) custom-call(s32[8,128]{1,0:T(8,128)S(1)} %broadcast_select_fusion.tags, f32[2,16,8,11]{3,2,1,0:T(8,128)S(1)} %bitcast.21, f32[3,4,16,8,128]{4,3,2,1,0:T(8,128)S(1)} %bitcast.18), custom_call_target="tpu_custom_call" | custom-call | tf_op jit(solution)/shard_map/pallas_call | solution.py:138
  15.7 0.0 copy-done.6
  15.7 0.0 copy-done.1
  15.7 0.0 copy-start.4
  15.8 3.2 %shard_map.67.acc = f32[11,4,16,8,128]{4,3,2,1,0:T(8,128)S(1)} custom-call(f32[11]{0:T(128)S(1)} %copy-done.6, f32[11,16,8,128]{3,2,1,0:T(8,128)S(1)} %get-tuple-element.31.edge, f32[11,4,16,8,128]{4,3,2,1,0:T(8,128)S(1)} %bitcast.14, f32[3,4,16,8,128]{4,3,2,1,0:T(8,128)S(1)} %get-tuple-element.30.va, f32[4,4,4,8,128]{4,3,2,1,0:T(8,128)S(1)} %get-tuple-element.32.cax, ...), custom_call_target="tpu_custom_call" | custom-call | tf_op jit(solution)/shard_map/pallas_call | solution.py:200
  18.9 2.3 %collective-permute-done.1.above = f32[12,16,128]{2,1,0:T(8,128)S(1)} collective-permute-done((f32[12,16,128]{2,1,0:T(8,128)S(1)}, f32[12,16,128]{2,1,0:T(8,128)S(1)}, u32[]{:S(2)}, u32[]{:S(2)}) %collective-permute-start.1) | collective-permute-done | bytes 98336 | tf_op jit(solution)/shard_map/ppermute | solution.py:445
  21.3 4.1 %collective-permute-done.below = f32[12,16,128]{2,1,0:T(8,128)S(1)} collective-permute-done((f32[12,16,128]{2,1,0:T(8,128)S(1)}, f32[12,16,128]{2,1,0:T(8,128)S(1)}, u32[]{:S(2)}, u32[]{:S(2)}) %collective-permute-start) | collective-permute-done | bytes 98336 | tf_op jit(solution)/shard_map/ppermute | solution.py:445
  25.4 0.0 copy-done.4
  25.4 0.0 collective-permute-done.2.below
  25.4 0.0 collective-permute-done.3.above
  25.5 0.9 %shard_map.68 = (f32[11,4,16,8,128]{4,3,2,1,0:T(8,128)S(1)}, f32[11,16,8,128]{3,2,1,0:T(8,128)S(1)}, f32[11,16,8,128]{3,2,1,0:T(8,128)S(1)}, f32[11,16,128]{2,1,...) custom-call(f32[11,16,128]{2,1,0:T(8,128)S(1)} %get-tuple-element.26.lo, ...), custom_call_target="tpu_custom_call", output_to_operand_aliasing={{0}: (6, {})} | custom-call | tf_op jit(solution)/shard_map/pallas_call | solution.py:343
  26.3 0.1 collective-permute-start.6
  26.4 1.3 %collective-permute-start.7 = (f32[11,16,8,128]{3,2,1,0:T(8,128)S(1)}, f32[11,16,8,128]{3,2,1,0:T(8,128)S(1)}, u32[]{:S(2)}, u32[]{:S(2)}) collective-permute-start(f32[11,16,8,128]{3,2,1,0:T(8,128)S(1)} %get-tuple-element.40), channel_id=1, source_target_pairs={{0,120},{8,16},{16,8},{24,32},{32,24},{40,48},{48,40},{56,64},{64,... | collective-permute-start | bytes 2162696 | tf_op jit(solution)/shard_map/ppermute | solution.py:452
  27.7 1.7 %collective-permute-start.5 = (f32[11,16,128]{2,1,0:T(8,128)S(1)}, f32[11,16,128]{2,1,0:T(8,128)S(1)}, u32[]{:S(2)}, u32[]{:S(2)}) collective-permute-start(f32[11,16,128]{2,1,0:T(8,128)S(1)} %get-tuple-element.34.own_low), channel_id=1, source_target_pairs={{1,0},{2,1},{3,2},{4,3},{5,4},{6,5},{7,6},{0,7},{9,8},{10,9},{11,1... | collective-permute-start | bytes 270344 | tf_op jit(solution)/shard_map/ppermute | solution.py:445
  29.4 0.4 collective-permute-start.4
  29.8 3.5 %shard_map.70.part = f32[11,4,16,8,128]{4,3,2,1,0:T(8,128)S(1)} custom-call(f32[11]{0:T(128)S(1)} %copy-done.6, f32[11,16,8,128]{3,2,1,0:T(8,128)S(1)} %get-tuple-element.31.edge, f32[11,4,16,8,128]{4,3,2,1,0:T(8,128)S(1)} %bitcast.16, f32[11,4,16,8,128]{4,3,2,1,0:T(8,128)S(1)} %get-tuple-element.42.s1, f32[3,4,16,8,128]{4,3,2,1,0:T(8,128)S(1)} %get-tuple-element.30.va, ...), custom_call_target="tpu_custom_call" | custom-call | tf_op jit(solution)/shard_map/pallas_call | solution.py:236
  33.3 5.2 %collective-permute-done.5.above = f32[11,16,128]{2,1,0:T(8,128)S(1)} collective-permute-done((f32[11,16,128]{2,1,0:T(8,128)S(1)}, f32[11,16,128]{2,1,0:T(8,128)S(1)}, u32[]{:S(2)}, u32[]{:S(2)}) %collective-permute-start.5) | collective-permute-done | bytes 90144 | tf_op jit(solution)/shard_map/ppermute | solution.py:445
  38.5 3.1 %collective-permute-done.4.below = f32[11,16,128]{2,1,0:T(8,128)S(1)} collective-permute-done((f32[11,16,128]{2,1,0:T(8,128)S(1)}, f32[11,16,128]{2,1,0:T(8,128)S(1)}, u32[]{:S(2)}, u32[]{:S(2)}) %collective-permute-start.4) | collective-permute-done | bytes 90144 | tf_op jit(solution)/shard_map/ppermute | solution.py:445
  41.6 0.0 collective-permute-done.6.chip
  41.6 0.0 collective-permute-done.7.cross
  41.6 2.0 %shard_map.71 = f32[11,4,16,8,128]{4,3,2,1,0:T(8,128)} custom-call(f32[11,16,128]{2,1,0:T(8,128)S(1)} %get-tuple-element.37.low, f32[11,16,128]{2,1,0:T(8,128)S(1)} %get-tuple-element.38.high, f32[11,16,8,128]{3,2,1,0:T(8,128)S(1)} %collective-permute-done.6.chip, f32[11,16,8,128]{3,2,1,0:T(8,128)S(1)} %collective-permute-done.7.cross, ...), custom_call_target="tpu_custom_call" | custom-call | tf_op jit(solution)/shard_map/pallas_call | solution.py:428
  (4 shorter events, 0.1 us)
Async XLA Ops:
  0.0 12.7 %copy-start.7 = (s32[2,1,8]{2,1,0:T(1,128)S(1)}, s32[2,1,8]{2,1,0:T(1,128)}, u32[]{:S(2)}) copy-start(s32[2,1,8]{2,1,0:T(1,128)} %param.10) | copy-start | bytes 196
  0.0 15.7 %copy-start.6 = (f32[11]{0:T(128)S(1)}, f32[11]{0:T(128)}, u32[]{:S(2)}) copy-start(f32[11]{0:T(128)} %decay.3) | copy-start | bytes 136
  0.0 1.8 %copy-start = (f32[11,4,4,4,1,8,128]{6,5,4,3,2,1,0:T(8,128)S(1)}, f32[11,4,4,4,1,8,128]{6,5,4,3,2,1,0:T(8,128)}, u32[]{:S(2)}) copy-start(f32[11,4,4,4,1,8,128]{6,5,4,3,2,1,0:T(8,128)} %param.6) | copy-start | bytes 8650756
  1.8 1.1 %copy-start.2 = (f32[3,4,4,4,1,8,128]{6,5,4,3,2,1,0:T(8,128)S(1)}, f32[3,4,4,4,1,8,128]{6,5,4,3,2,1,0:T(8,128)}, u32[]{:S(2)}) copy-start(f32[3,4,4,4,1,8,128]{6,5,4,3,2,1,0:T(8,128)} %param.7) | copy-start | bytes 2359300
  3.0 9.8 %copy-start.3 = (f32[3,4,4,4,1,8,128]{6,5,4,3,2,1,0:T(8,128)S(1)}, f32[3,4,4,4,1,8,128]{6,5,4,3,2,1,0:T(8,128)}, u32[]{:S(2)}) copy-start(f32[3,4,4,4,1,8,128]{6,5,4,3,2,1,0:T(8,128)} %param.7) | copy-start | bytes 2359300
  3.0 12.8 %copy-start.1 = (f32[11,4,4,4,1,8,128]{6,5,4,3,2,1,0:T(8,128)S(1)}, f32[11,4,4,4,1,8,128]{6,5,4,3,2,1,0:T(8,128)}, u32[]{:S(2)}) copy-start(f32[11,4,4,4,1,8,128]{6,5,4,3,2,1,0:T(8,128)} %param.6) | copy-start | bytes 8650756
  3.2 22.2 %collective-permute-start.2 = (f32[12,16,8,128]{3,2,1,0:T(8,128)S(1)}, f32[12,16,8,128]{3,2,1,0:T(8,128)S(1)}, u32[]{:S(2)}, u32[]{:S(2)}) collective-permute-start(f32[12,16,8,128]{3,2,1,0:T(8,128)S(1)} %get-tuple-element.28), channel_id=1, source_target_pairs={{0,8},{8,16},{16,24},{24,32},{32,40},{40,48},{48,56},{56,64},{64,7... | collective-permute-start | bytes 2359304 | tf_op jit(solution)/shard_map/ppermute | solution.py:445
  3.3 22.1 %collective-permute-start.3 = (f32[12,16,8,128]{3,2,1,0:T(8,128)S(1)}, f32[12,16,8,128]{3,2,1,0:T(8,128)S(1)}, u32[]{:S(2)}, u32[]{:S(2)}) collective-permute-start(f32[12,16,8,128]{3,2,1,0:T(8,128)S(1)} %get-tuple-element.29), channel_id=1, source_target_pairs={{8,0},{16,8},{24,16},{32,24},{40,32},{48,40},{56,48},{64,56},{72,6... | collective-permute-start | bytes 2359304 | tf_op jit(solution)/shard_map/ppermute | solution.py:445
  9.4 11.8 %collective-permute-start.1 = (f32[12,16,128]{2,1,0:T(8,128)S(1)}, f32[12,16,128]{2,1,0:T(8,128)S(1)}, u32[]{:S(2)}, u32[]{:S(2)}) collective-permute-start(f32[12,16,128]{2,1,0:T(8,128)S(1)} %get-tuple-element.24.own_low), channel_id=1, source_target_pairs={{1,0},{2,1},{3,2},{4,3},{5,4},{6,5},{7,6},{0,7},{9,8},{10,9},{11,1... | collective-permute-start | bytes 294920 | tf_op jit(solution)/shard_map/ppermute | solution.py:445
  12.7 12.7 %collective-permute-start = (f32[12,16,128]{2,1,0:T(8,128)S(1)}, f32[12,16,128]{2,1,0:T(8,128)S(1)}, u32[]{:S(2)}, u32[]{:S(2)}) collective-permute-start(f32[12,16,128]{2,1,0:T(8,128)S(1)} %get-tuple-element.25.own_high), channel_id=1, source_target_pairs={{0,1},{1,2},{2,3},{3,4},{4,5},{5,6},{6,7},{7,0},{8,9},{9,10},{10,1... | collective-permute-start | bytes 294920 | tf_op jit(solution)/shard_map/ppermute | solution.py:445
  12.8 0.9 %copy-start.5 = (f32[2,11,4,4,1,8]{1,5,4,3,2,0:T(8,128)S(1)}, f32[2,11,4,4,1,8]{1,5,4,3,2,0:T(8,128)}, u32[]{:S(2)}) copy-start(f32[2,11,4,4,1,8]{1,5,4,3,2,0:T(8,128)} %param.9) | copy-start | bytes 33796
  15.7 9.6 %copy-start.4 = (f32[11,4,4,1,128]{4,3,2,1,0:T(1,128)S(1)}, f32[11,4,4,1,128]{4,3,2,1,0:T(1,128)}, u32[]{:S(2)}) copy-start(f32[11,4,4,1,128]{4,3,2,1,0:T(1,128)} %param.8) | copy-start | bytes 270340
  26.3 15.3 %collective-permute-start.6 = (f32[11,16,8,128]{3,2,1,0:T(8,128)S(1)}, f32[11,16,8,128]{3,2,1,0:T(8,128)S(1)}, u32[]{:S(2)}, u32[]{:S(2)}) collective-permute-start(f32[11,16,8,128]{3,2,1,0:T(8,128)S(1)} %get-tuple-element.39), channel_id=1, source_target_pairs={{0,8},{8,0},{16,24},{24,16},{32,40},{40,32},{48,56},{56,48},{64,72... | collective-permute-start | bytes 2162696 | tf_op jit(solution)/shard_map/ppermute | solution.py:452
  26.4 15.2 %collective-permute-start.7 = (f32[11,16,8,128]{3,2,1,0:T(8,128)S(1)}, f32[11,16,8,128]{3,2,1,0:T(8,128)S(1)}, u32[]{:S(2)}, u32[]{:S(2)}) collective-permute-start(f32[11,16,8,128]{3,2,1,0:T(8,128)S(1)} %get-tuple-element.40), channel_id=1, source_target_pairs={{0,120},{8,16},{16,8},{24,32},{32,24},{40,48},{48,40},{56,64},{64,... | collective-permute-start | bytes 2162696 | tf_op jit(solution)/shard_map/ppermute | solution.py:452
  27.7 10.8 %collective-permute-start.5 = (f32[11,16,128]{2,1,0:T(8,128)S(1)}, f32[11,16,128]{2,1,0:T(8,128)S(1)}, u32[]{:S(2)}, u32[]{:S(2)}) collective-permute-start(f32[11,16,128]{2,1,0:T(8,128)S(1)} %get-tuple-element.34.own_low), channel_id=1, source_target_pairs={{1,0},{2,1},{3,2},{4,3},{5,4},{6,5},{7,6},{0,7},{9,8},{10,9},{11,1... | collective-permute-start | bytes 270344 | tf_op jit(solution)/shard_map/ppermute | solution.py:445
  29.4 12.2 %collective-permute-start.4 = (f32[11,16,128]{2,1,0:T(8,128)S(1)}, f32[11,16,128]{2,1,0:T(8,128)S(1)}, u32[]{:S(2)}, u32[]{:S(2)}) collective-permute-start(f32[11,16,128]{2,1,0:T(8,128)S(1)} %get-tuple-element.35.own_high), channel_id=1, source_target_pairs={{0,1},{1,2},{2,3},{3,4},{4,5},{5,6},{6,7},{7,0},{8,9},{9,10},{10,1... | collective-permute-start | bytes 270344 | tf_op jit(solution)/shard_map/ppermute | solution.py:445
